TPU v7x, 32 devices: a whole 2x2x4 slice. The times are simulated.
32 devices in a mesh: dp: 8 (over y, x, core), fsdp: 4 (over z).
Axes of the slice: x: 2, y: 2, z: 4, core: 2. Of those that a mesh axis runs over, the one named last changes fastest.
Arguments:
- tokens: bfloat16 [32768, 768], P(('dp', 'fsdp')), may hold values from -6 to 6
- lengths: int32 [32], P(('dp', 'fsdp')), may hold values from 1 to 1024, 24576 in all
- cotangent: bfloat16 [32768, 768], P(('dp', 'fsdp')), may hold values from -6 to 6
- project_weight: bfloat16 [768, 2304], P('dp', 'fsdp'), may hold values from -0.21875 to 0.21875
- project_bias: bfloat16 [1536], P('dp'), may hold values from -1.1953125 to 1.1953125
- output_weight: bfloat16 [768, 768], P('dp', 'fsdp'), may hold values from -3.5 to 3.5
- output_bias: bfloat16 [768], P('dp'), may hold values from -1.1953125 to 1.1953125
- expand_weight: bfloat16 [768, 3072], P('dp', 'fsdp'), may hold values from -0.21875 to 0.21875
- expand_bias: bfloat16 [3072], P('dp'), may hold values from -1.1953125 to 1.1953125
- contract_weight: bfloat16 [3072, 768], P('dp', 'fsdp'), may hold values from -0.109375 to 0.109375
- contract_bias: bfloat16 [768], P('dp'), may hold values from -1.1953125 to 1.1953125
- first_gain: bfloat16 [768], P('dp'), may hold values from 0.25 to 1.75
- first_shift: bfloat16 [768], P('dp'), may hold values from -1.1953125 to 1.1953125
- second_gain: bfloat16 [768], P('dp'), may hold values from 0.25 to 1.75
- second_shift: bfloat16 [768], P('dp'), may hold values from -1.1953125 to 1.1953125
Outputs:
- block_out: bfloat16 [32768, 768], P(('dp', 'fsdp'))
- tokens_grad: bfloat16 [32768, 768], P(('dp', 'fsdp'))
- project_weight_grad: float32 [768, 2304], P('dp', 'fsdp')
- project_bias_grad: float32 [1536], P('dp')
- output_weight_grad: float32 [768, 768], P('dp', 'fsdp')
- output_bias_grad: float32 [768], P('dp')
- expand_weight_grad: float32 [768, 3072], P('dp', 'fsdp')
- expand_bias_grad: float32 [3072], P('dp')
- contract_weight_grad: float32 [3072, 768], P('dp', 'fsdp')
- contract_bias_grad: float32 [768], P('dp')
- first_gain_grad: float32 [768], P('dp')
- first_shift_grad: float32 [768], P('dp')
- second_gain_grad: float32 [768], P('dp')
- second_shift_grad: float32 [768], P('dp')
Inputs may be any that keep to these rules, and one draw needn't show every extreme that they name: `lengths`: each cell's number of live tokens; some cell has exactly 1024.
All inputs are finite; a program needn't handle non-finite values. No bound on the sum of `lengths` on one device may be relied on, other than what follows from the above.
Results may differ from a plain program's by a relative error of at most 0.013.
Values may be sent and summed in bfloat16 or wider, within the bound.
A program may use at most 256 MiB of HBM per device.

v0:
```python
import jax
import jax.numpy as jnp
from jax import lax
from jax.sharding import PartitionSpec as P

H = 12
HD = 64


eps_norm = 1e-05
neg_fill = -1000000000.0


def layer_norm(values, gain_row, shift_row):
    centre = jnp.mean(values, axis=-1, keepdims=True)
    centred = values - centre
    spread = jnp.mean(centred * centred, axis=-1, keepdims=True)
    return centred * lax.rsqrt(spread + eps_norm) * gain_row + shift_row


def gelu_exact(values):
    return jax.nn.gelu(values, approximate=False)


def matmul(first, second):
    return jnp.dot(first, second, preferred_element_type=jnp.float32)


def over_rows(first, second):
    return lax.dot_general(
        first, second, (((0,), (0,)), ((), ())), preferred_element_type=jnp.float32
    )


def over_columns(first, second):
    return lax.dot_general(
        first, second, (((1,), (1,)), ((), ())), preferred_element_type=jnp.float32
    )


def fetch_forward(
    project_weight,
    output_weight,
    expand_weight,
    contract_weight,
    project_bias,
    output_bias,
    expand_bias,
    contract_bias,
    first_gain,
    first_shift,
    second_gain,
    second_shift,
):
    wide_project, wide_output, wide_expand, wide_contract = (
        lax.all_gather(project_weight, "fsdp", axis=1, tiled=True),
        lax.all_gather(output_weight, "fsdp", axis=1, tiled=True),
        lax.all_gather(expand_weight, "fsdp", axis=1, tiled=True),
        lax.all_gather(contract_weight, "fsdp", axis=1, tiled=True),
    )
    return (
        lax.all_gather(wide_project, "dp", axis=0, tiled=True),
        lax.all_gather(wide_output, "dp", axis=0, tiled=True),
        lax.all_gather(wide_expand, "dp", axis=0, tiled=True),
        lax.all_gather(wide_contract, "dp", axis=0, tiled=True),
        lax.all_gather(project_bias, "dp", axis=0, tiled=True),
        lax.all_gather(output_bias, "dp", axis=0, tiled=True),
        lax.all_gather(expand_bias, "dp", axis=0, tiled=True),
        lax.all_gather(contract_bias, "dp", axis=0, tiled=True),
        lax.all_gather(first_gain, "dp", axis=0, tiled=True),
        lax.all_gather(first_shift, "dp", axis=0, tiled=True),
        lax.all_gather(second_gain, "dp", axis=0, tiled=True),
        lax.all_gather(second_shift, "dp", axis=0, tiled=True),
    )


def fetch_backward(
    project_weight,
    output_weight,
    expand_weight,
    contract_weight,
    project_bias,
    output_bias,
    expand_bias,
    contract_bias,
    first_gain,
    first_shift,
    second_gain,
    second_shift,
):
    wide_project, wide_output, wide_expand, wide_contract = (
        lax.all_gather(project_weight, "fsdp", axis=1, tiled=True),
        lax.all_gather(output_weight, "fsdp", axis=1, tiled=True),
        lax.all_gather(expand_weight, "fsdp", axis=1, tiled=True),
        lax.all_gather(contract_weight, "fsdp", axis=1, tiled=True),
    )
    return (
        lax.all_gather(wide_project, "dp", axis=0, tiled=True),
        lax.all_gather(wide_output, "dp", axis=0, tiled=True),
        lax.all_gather(wide_expand, "dp", axis=0, tiled=True),
        lax.all_gather(wide_contract, "dp", axis=0, tiled=True),
        lax.all_gather(project_bias, "dp", axis=0, tiled=True),
        lax.all_gather(output_bias, "dp", axis=0, tiled=True),
        lax.all_gather(expand_bias, "dp", axis=0, tiled=True),
        lax.all_gather(contract_bias, "dp", axis=0, tiled=True),
        lax.all_gather(first_gain, "dp", axis=0, tiled=True),
        lax.all_gather(first_shift, "dp", axis=0, tiled=True),
        lax.all_gather(second_gain, "dp", axis=0, tiled=True),
        lax.all_gather(second_shift, "dp", axis=0, tiled=True),
    )


def split_heads(cell_rows, block_rows):
    slot_count = cell_rows.shape[0]
    width = cell_rows.shape[1] // 3
    query_blocks = cell_rows[:, :width].reshape(slot_count // block_rows, block_rows, H, HD)
    keys_all = cell_rows[:, width : 2 * width].reshape(slot_count, H, HD)
    values_all = cell_rows[:, 2 * width :].reshape(slot_count, H, HD)
    return (query_blocks, keys_all, values_all)


def block_scores(query_block, keys_all, key_live):
    scores = jnp.einsum(
        "qhe,khe->hqk", query_block, keys_all, preferred_element_type=jnp.float32
    ) * HD ** (-0.5)
    return jnp.where(key_live[None, None, :], scores, neg_fill)


def attend_forward(query_block, keys_all, values_all, key_live):
    scores = block_scores(query_block, keys_all, key_live)
    row_max = jnp.max(scores, axis=-1, keepdims=True)
    powers = jnp.exp(scores - row_max)
    row_total = jnp.sum(powers, axis=-1, keepdims=True)
    weights = (powers / row_total).astype(jnp.bfloat16)
    mixed_block = jnp.einsum(
        "hqk,khe->qhe", weights, values_all, preferred_element_type=jnp.float32
    )
    return (mixed_block, (row_max + jnp.log(row_total))[:, :, 0])


def attend_backward(query_block, grad_block, log_block, keys_all, values_all, key_live):
    scores = block_scores(query_block, keys_all, key_live)
    weights = jnp.exp(scores - log_block[:, :, None])
    grad_weights = jnp.einsum(
        "qhe,khe->hqk", grad_block, values_all, preferred_element_type=jnp.float32
    )
    row_inner = jnp.sum(grad_weights * weights, axis=-1, keepdims=True)
    grad_scores = (weights * (grad_weights - row_inner)).astype(jnp.bfloat16)
    grad_query = jnp.einsum(
        "hqk,khe->qhe", grad_scores, keys_all, preferred_element_type=jnp.float32
    ) * HD ** (-0.5)
    grad_key = jnp.einsum(
        "hqk,qhe->khe", grad_scores, query_block, preferred_element_type=jnp.float32
    ) * HD ** (-0.5)
    grad_value = jnp.einsum(
        "hqk,qhe->khe", weights.astype(jnp.bfloat16), grad_block, preferred_element_type=jnp.float32
    )
    return (grad_query, grad_key, grad_value)


def per_device(
    tokens,
    lengths,
    cotangent,
    project_weight,
    project_bias,
    output_weight,
    output_bias,
    expand_weight,
    expand_bias,
    contract_weight,
    contract_bias,
    first_gain,
    first_shift,
    second_gain,
    second_shift,
):
    fetched = fetch_forward(
        project_weight,
        output_weight,
        expand_weight,
        contract_weight,
        project_bias,
        output_bias,
        expand_bias,
        contract_bias,
        first_gain,
        first_shift,
        second_gain,
        second_shift,
    )
    full_project, full_output, full_expand, full_contract = (
        fetched[0],
        fetched[1],
        fetched[2],
        fetched[3],
    )
    vectors = [item.astype(jnp.float32) for item in fetched[4:]]
    bias_project, bias_output, bias_expand, bias_contract = (
        vectors[0],
        vectors[1],
        vectors[2],
        vectors[3],
    )
    gain_one, shift_one, gain_two, shift_two = (vectors[4], vectors[5], vectors[6], vectors[7])
    cell_count = lengths.shape[0]
    slot_count = tokens.shape[0] // cell_count
    width = tokens.shape[1]
    block_rows = min(512, slot_count)
    positions = jnp.arange(slot_count, dtype=jnp.int32)
    live_keys = positions[None, :] < lengths[:, None]
    live_rows = live_keys.reshape(-1)
    rows_in = tokens.astype(jnp.float32)
    normed_one = layer_norm(rows_in, gain_one, shift_one).astype(jnp.bfloat16)
    bias_full = jnp.concatenate(
        [bias_project[:width], jnp.zeros((width,), jnp.float32), bias_project[width:]]
    )
    projected = (matmul(normed_one, full_project) + bias_full).astype(jnp.bfloat16)
    cell_index = 0
    query_blocks, keys_all, values_all = split_heads(projected, block_rows)
    key_live = live_keys[cell_index]
    mixed_blocks, log_blocks = lax.map(
        lambda query_block: attend_forward(query_block, keys_all, values_all, key_live),
        query_blocks,
    )
    mixed_list = mixed_blocks.reshape(slot_count, width)
    log_list = [log_blocks]
    mixed_low = mixed_list.astype(jnp.bfloat16)
    middle = rows_in + (matmul(mixed_low, full_output) + bias_output)
    normed_two = layer_norm(middle, gain_two, shift_two).astype(jnp.bfloat16)
    hidden = matmul(normed_two, full_expand) + bias_expand
    active = gelu_exact(hidden).astype(jnp.bfloat16)
    result = middle + (matmul(active, full_contract) + bias_contract)
    block_out = jnp.where(live_rows[:, None], result, 0.0).astype(jnp.bfloat16)
    again = fetch_backward(
        project_weight,
        output_weight,
        expand_weight,
        contract_weight,
        project_bias,
        output_bias,
        expand_bias,
        contract_bias,
        first_gain,
        first_shift,
        second_gain,
        second_shift,
    )
    back_project, back_output, back_expand, back_contract = (again[0], again[1], again[2], again[3])
    grad_out = jnp.where(live_rows[:, None], cotangent.astype(jnp.float32), 0.0)
    grad_out_low = grad_out.astype(jnp.bfloat16)
    grad_contract = over_rows(active, grad_out_low)
    grad_contract_bias = jnp.sum(grad_out, axis=0)
    grad_active = over_columns(grad_out_low, back_contract)
    gelu_value, gelu_pull = jax.vjp(gelu_exact, hidden)
    grad_hidden = gelu_pull(grad_active)[0].astype(jnp.bfloat16)
    grad_expand = over_rows(normed_two, grad_hidden)
    grad_expand_bias = jnp.sum(grad_hidden.astype(jnp.float32), axis=0)
    grad_normed_two = over_columns(grad_hidden, back_expand)
    norm_value, second_pull = jax.vjp(layer_norm, middle, gain_two, shift_two)
    grad_middle, grad_gain_two, grad_shift_two = second_pull(grad_normed_two)
    grad_middle = grad_middle + grad_out
    grad_branch = grad_middle.astype(jnp.bfloat16)
    grad_output = over_rows(mixed_low, grad_branch)
    grad_output_bias = jnp.sum(grad_branch.astype(jnp.float32), axis=0)
    grad_mixed = over_columns(grad_branch, back_output).astype(jnp.bfloat16)
    cell_index = 0
    query_blocks, keys_all, values_all = split_heads(projected, block_rows)
    key_live = live_keys[cell_index]
    grad_blocks = grad_mixed.reshape(slot_count // block_rows, block_rows, H, HD)

    def visit_block(carried, inputs):
        query_block, grad_block, log_block = inputs
        grad_query, grad_key, grad_value = attend_backward(
            query_block, grad_block, log_block, keys_all, values_all, key_live
        )
        return ((carried[0] + grad_key, carried[1] + grad_value), grad_query)

    initial = (
        jnp.zeros((slot_count, H, HD), jnp.float32),
        jnp.zeros((slot_count, H, HD), jnp.float32),
    )
    (key_sums, value_sums), query_grads = lax.scan(
        visit_block, initial, (query_blocks, grad_blocks, log_list[cell_index])
    )
    grad_cells = jnp.concatenate(
        [
            query_grads.reshape(slot_count, width),
            key_sums.reshape(slot_count, width),
            value_sums.reshape(slot_count, width),
        ],
        axis=1,
    )
    grad_projected = grad_cells.astype(jnp.bfloat16)
    grad_project = over_rows(normed_one, grad_projected)
    column_sums = jnp.sum(grad_projected.astype(jnp.float32), axis=0)
    grad_project_bias = jnp.concatenate([column_sums[:width], column_sums[2 * width :]])
    grad_normed_one = over_columns(grad_projected, back_project)
    first_value, first_pull = jax.vjp(layer_norm, rows_in, gain_one, shift_one)
    grad_rows_in, grad_gain_one, grad_shift_one = first_pull(grad_normed_one)
    tokens_grad = (grad_rows_in + grad_middle).astype(jnp.bfloat16)
    reduced = (
        lax.psum_scatter(grad_project, "dp", scatter_dimension=0, tiled=True),
        lax.psum_scatter(grad_output, "dp", scatter_dimension=0, tiled=True),
        lax.psum_scatter(grad_expand, "dp", scatter_dimension=0, tiled=True),
        lax.psum_scatter(grad_contract, "dp", scatter_dimension=0, tiled=True),
        lax.psum_scatter(grad_project_bias, "dp", scatter_dimension=0, tiled=True),
        lax.psum_scatter(grad_output_bias, "dp", scatter_dimension=0, tiled=True),
        lax.psum_scatter(grad_expand_bias, "dp", scatter_dimension=0, tiled=True),
        lax.psum_scatter(grad_contract_bias, "dp", scatter_dimension=0, tiled=True),
        lax.psum_scatter(grad_gain_one, "dp", scatter_dimension=0, tiled=True),
        lax.psum_scatter(grad_shift_one, "dp", scatter_dimension=0, tiled=True),
        lax.psum_scatter(grad_gain_two, "dp", scatter_dimension=0, tiled=True),
        lax.psum_scatter(grad_shift_two, "dp", scatter_dimension=0, tiled=True),
    )
    shard_project, shard_output, shard_expand, shard_contract = (
        lax.psum_scatter(
            reduced[0].astype(jnp.bfloat16), "fsdp", scatter_dimension=1, tiled=True
        ).astype(jnp.float32),
        lax.psum_scatter(
            reduced[1].astype(jnp.bfloat16), "fsdp", scatter_dimension=1, tiled=True
        ).astype(jnp.float32),
        lax.psum_scatter(
            reduced[2].astype(jnp.bfloat16), "fsdp", scatter_dimension=1, tiled=True
        ).astype(jnp.float32),
        lax.psum_scatter(
            reduced[3].astype(jnp.bfloat16), "fsdp", scatter_dimension=1, tiled=True
        ).astype(jnp.float32),
    )
    summed = lax.psum(
        (
            reduced[4],
            reduced[5],
            reduced[6],
            reduced[7],
            reduced[8],
            reduced[9],
            reduced[10],
            reduced[11],
        ),
        "fsdp",
    )
    return (
        block_out,
        tokens_grad,
        shard_project,
        summed[0],
        shard_output,
        summed[1],
        shard_expand,
        summed[2],
        shard_contract,
        summed[3],
        summed[4],
        summed[5],
        summed[6],
        summed[7],
    )


def solution(mesh):
    placed = (
        P(("dp", "fsdp"), None),
        P(("dp", "fsdp")),
        P(("dp", "fsdp"), None),
        P("dp", "fsdp"),
        P("dp"),
        P("dp", "fsdp"),
        P("dp"),
        P("dp", "fsdp"),
        P("dp"),
        P("dp", "fsdp"),
        P("dp"),
        P("dp"),
        P("dp"),
        P("dp"),
        P("dp"),
    )
    return jax.shard_map(
        per_device,
        mesh=mesh,
        in_specs=placed,
        out_specs=(
            P(("dp", "fsdp"), None),
            P(("dp", "fsdp"), None),
            P("dp", "fsdp"),
            P("dp"),
            P("dp", "fsdp"),
            P("dp"),
            P("dp", "fsdp"),
            P("dp"),
            P("dp", "fsdp"),
            P("dp"),
            P("dp"),
            P("dp"),
            P("dp"),
            P("dp"),
        ),
        check_vma=False,
    )
```

profile of v0, /device:TPU:0, one launch (start us, length us, event | category | flops | bytes accessed | tf_op | source)
XLA Modules:
  0.0 822.7 jit_solution(3698584728035570422)
XLA Ops:
  7.3 17.3 %all-gather = bf16[4,576,96]{1,2,0:T(8,128)(2,1)S(1)} all-gather(bf16[1,576,96]{1,2,0:T(8,128)(2,1)} %bitcast.149), channel_id=1, replica_groups=mesh['dp'=8,'fsdp'=4] {'fsdp'}, dimensions={0}, use_global_device_ids=true | all-gather | bytes 552960 | tf_op jit(solution)/shard_map/all_gather | solution.py:56
  27.1 14.0 %all_gather.61 = bf16[96,768]{0,1:T(8,128)(2,1)S(1)} all-gather(bf16[96,192]{0,1:T(8,128)(2,1)S(1)} %copy.94), channel_id=1, replica_groups=mesh['dp'=8,'fsdp'=4] {'fsdp'}, dimensions={1}, use_global_device_ids=true | all-gather | bytes 184320 | tf_op jit(solution)/shard_map/all_gather | solution.py:57
  42.0 17.8 %all_gather.66 = bf16[96,3072]{1,0:T(8,128)(2,1)} all-gather(bf16[96,768]{1,0:T(8,128)(2,1)S(1)} %copy-done.22), channel_id=1, replica_groups=mesh['dp'=8,'fsdp'=4] {'fsdp'}, dimensions={1}, use_global_device_ids=true | all-gather | bytes 737280 | tf_op jit(solution)/shard_map/all_gather | solution.py:58
  59.9 15.9 %all_gather.69 = bf16[384,768]{0,1:T(8,128)(2,1)} all-gather(bf16[384,192]{0,1:T(8,128)(2,1)S(1)} %copy-done.23), channel_id=1, replica_groups=mesh['dp'=8,'fsdp'=4] {'fsdp'}, dimensions={1}, use_global_device_ids=true | all-gather | bytes 737280 | tf_op jit(solution)/shard_map/all_gather | solution.py:59
  80.7 23.2 %all-reduce.17 = (bf16[1536]{0:T(1024)(128)(2,1)S(1)}, bf16[768]{0:T(1024)(128)(2,1)S(1)}, bf16[768]{0:T(1024)(128)(2,1)S(1)}, bf16[768]{0:T(1024)(128)(2,1)S(1)...) all-reduce(bf16[1536]{0:T(1024)(128)(2,1)S(1)} %dynamic-update-slic, ...), channel_id=1, replica_groups=mesh['dp'=8,'fsdp'=4] {'dp'}, use_global_device_ids=true, to_apply=%add.2 | all-reduce | flops 6144 | bytes 24576
  105.7 8.5 %all-gather.1 = bf16[8,1,384]{2,1,0:T(2,128)(2,1)S(1)} all-gather(bf16[1,1,384]{2,1,0:T(2,128)(2,1)S(1)} %reshape.198), channel_id=1, replica_groups=mesh['dp'=8,'fsdp'=4] {'dp'}, dimensions={0}, use_global_device_ids=true | all-gather | bytes 6912 | tf_op jit(solution)/shard_map/all_gather | solution.py:68
  119.3 6.4 add_convert_fusion.1
  132.2 3.8 reshape.168
  139.0 70.6 %while.28 = (s32[]{:T(128)}, bf16[2,512,12,64]{1,3,2,0:T(8,128)(2,1)}, f32[2,12,512]{2,1,0:T(8,128)S(1)}, bf16[2,512,12,64]{1,3,2,0:T(8,128)(2,1)S(1)}, bf16[102...) while((s32[]{:T(128)}, ...), condition=%wide.region_5.6_spmd.clone, body=%wide.region_2.5_spmd.clone.sunk | while | flops 1686105088 | bytes 100118728 | solution.py:222
  139.7 10.2 %fusion.119 = (f32[12,512]{1,0:T(8,128)S(1)}, f32[12,512,1024]{2,1,0:T(8,128)}) fusion(pred[1024]{0:T(1024)(128)(4,1)S(1)} %compare_reduce_fusion.4, bf16[1024,12,64]{0,2,1:T(8,128)(2,1)S(1)} %get-tuple-element.511, bf16[2,512,12,64]{1,3,2,0:T(8,128)(2,1)S(1)} %get-tuple-element.510, s32[]{:T(128)S(6)} %copy.131), kind=kOutput, calls=%fused_computation.5.clone.1 | convolution fusion | flops 824174592 | bytes 27550724 | tf_op jit(solution)/shard_map/while/body/eval_jaxpr/qhe,khe->hqk/dot_general | solution.py:123
  149.9 12.0 %fusion.120 = f32[12,512]{1,0:T(8,128)S(1)} fusion(f32[12,512,1024]{2,1,0:T(8,128)} %get-tuple-element.477, f32[12,512]{1,0:T(8,128)S(1)} %get-tuple-element.478, pred[1024]{0:T(1024)(128)(4,1)S(1)} %compare_reduce_fusion.4), kind=kLoop, calls=%fused_computation.6.clone.1 | loop fusion | flops 25159680 | bytes 25216000 | tf_op jit(solution)/shard_map/while/body/eval_jaxpr/reduce_sum | solution.py:133
  161.9 11.6 %bitcast_dynamic-update-slice_fusion.6 = bf16[2,512,12,64]{1,3,2,0:T(8,128)(2,1)S(1)} fusion(bf16[2,512,12,64]{1,3,2,0:T(8,128)(2,1)S(1)} %copy-done.13, s32[]{:T(128)S(6)} %copy.131, bf16[1024,12,64]{0,2,1:T(8,128)(2,1)S(1)} %copy-done.1, f32[12,512,1024]{2,1,0:T(8,128)} %get-tuple-element.477, f32[12,512]{1,0:T(8,128)S(1)} %fusion.120, ...), kind=kOutput, calls=%fused_computation.8.clone.1 | convolution fusion | flops 836763648 | bytes 28378116 | tf_op jit(solution)/shard_map/while/body/eval_jaxpr/hqk,khe->qhe/dot_general | solution.py:135
  175.3 10.2 %fusion.119 = (f32[12,512]{1,0:T(8,128)S(1)}, f32[12,512,1024]{2,1,0:T(8,128)}) fusion(pred[1024]{0:T(1024)(128)(4,1)S(1)} %compare_reduce_fusion.4, bf16[1024,12,64]{0,2,1:T(8,128)(2,1)S(1)} %get-tuple-element.511, bf16[2,512,12,64]{1,3,2,0:T(8,128)(2,1)S(1)} %get-tuple-element.510, s32[]{:T(128)S(6)} %copy.131), kind=kOutput, calls=%fused_computation.5.clone.1 | convolution fusion | flops 824174592 | bytes 27550724 | tf_op jit(solution)/shard_map/while/body/eval_jaxpr/qhe,khe->hqk/dot_general | solution.py:123
  185.5 11.4 %fusion.120 = f32[12,512]{1,0:T(8,128)S(1)} fusion(f32[12,512,1024]{2,1,0:T(8,128)} %get-tuple-element.477, f32[12,512]{1,0:T(8,128)S(1)} %get-tuple-element.478, pred[1024]{0:T(1024)(128)(4,1)S(1)} %compare_reduce_fusion.4), kind=kLoop, calls=%fused_computation.6.clone.1 | loop fusion | flops 25159680 | bytes 25216000 | tf_op jit(solution)/shard_map/while/body/eval_jaxpr/reduce_sum | solution.py:133
  196.9 11.2 %bitcast_dynamic-update-slice_fusion.6 = bf16[2,512,12,64]{1,3,2,0:T(8,128)(2,1)S(1)} fusion(bf16[2,512,12,64]{1,3,2,0:T(8,128)(2,1)S(1)} %copy-done.13, s32[]{:T(128)S(6)} %copy.131, bf16[1024,12,64]{0,2,1:T(8,128)(2,1)S(1)} %copy-done.1, f32[12,512,1024]{2,1,0:T(8,128)} %get-tuple-element.477, f32[12,512]{1,0:T(8,128)S(1)} %fusion.120, ...), kind=kOutput, calls=%fused_computation.8.clone.1 | convolution fusion | flops 836763648 | bytes 28378116 | tf_op jit(solution)/shard_map/while/body/eval_jaxpr/hqk,khe->qhe/dot_general | solution.py:135
  209.6 3.0 copy.93
  214.3 3.9 fusion.76
  220.3 37.8 %multiply_convert_fusion.1 = (bf16[1024,3072]{1,0:T(8,128)(2,1)}, f32[1024,3072]{1,0:T(8,128)}, f32[1024,3072]{1,0:T(8,128)}) fusion(f32[3072]{0:T(1024)S(1)} %bitcast.151, bf16[768,3072]{1,0:T(8,128)(2,1)} %all-gather.11.cloned.1.call-done, f32[1024,768]{0,1:T(8,128)} %copy-done.7, f32[768]{0:T(1024)S(1)} %copy-done.44, f32[768]{0:T(1024)S(1)} %copy-done.34, ...), kind=kOutput, calls=%fused_computation.48 | convolution fusion | flops 5043388416 | bytes 39348224 | tf_op jit(solution)/shard_map/dot_general | solution.py:26
  258.1 20.3 %convert_reduce_fusion = (f32[3072]{0:T(1024)}, bf16[1024,3072]{1,0:T(8,128)(2,1)}) fusion(f32[1024,3072]{1,0:T(8,128)} %get-tuple-element.354, bf16[3072,768]{0,1:T(8,128)(2,1)} %all-gather.13.cloned.1.call-done, bf16[1024,768]{0,1:T(8,128)(2,1)} %copy.97, pred[1024]{0:T(1024)(128)(4,1)S(1)} %copy-done.50, f32[1024,3072]{1,0:T(8,128)} %get-tuple-element.372, ...), kind=kOutput, calls=%fused_computation.46 | convolution fusion | flops 4887671808 | bytes 37774336 | tf_op jit(solution)/shard_map/dot_general | solution.py:36
  278.4 9.0 %fusion.78 = (f32[768]{0:T(1024)}, f32[1024,768]{1,0:T(8,128)}) fusion(bf16[1024,3072]{1,0:T(8,128)(2,1)} %get-tuple-element.374, bf16[768,3072]{1,0:T(8,128)(2,1)S(1)} %copy-done.55), kind=kOutput, calls=%fused_computation.122 | convolution fusion | flops 4832623616 | bytes 14158848 | tf_op jit(solution)/shard_map/dot_general | solution.py:36
  287.4 3.6 copy.98
  291.0 4.5 multiply_reduce_fusion.1
  299.5 2.9 fusion.79
  302.4 4.3 convolution_convert_fusion
  306.7 2.6 copy.99
  309.3 3.8 reshape.171
  313.1 2.9 copy.101
  317.4 164.7 %while.29 = (s32[]{:T(128)}, f32[1024,12,64]{0,2,1:T(8,128)}, f32[1024,12,64]{0,2,1:T(8,128)}, bf16[2,512,12,64]{1,3,2,0:T(8,128)(2,1)}, bf16[2,512,12,64]{1,3,2...) while((s32[]{:T(128)}, f32[1024,12,64]{0,2,1:T(8,128)}, ...), condition=%wide.region_12.13_spmd.clone, body=%wide.region_10.12_spmd.clone.sunk | while | flops 4125223936 | bytes 217239728 | solution.py:283
  318.5 11.0 %fusion.130 = f32[12,512,1024]{2,1,0:T(8,128)} fusion(bf16[1024,12,64]{0,2,1:T(8,128)(2,1)S(1)} %get-tuple-element.544, bf16[2,512,12,64]{1,3,2,0:T(8,128)(2,1)S(1)} %get-tuple-element.543, s32[]{:T(128)S(6)} %copy.141), kind=kOutput, calls=%fused_computation.30.clone.1 | convolution fusion | flops 805306368 | bytes 27525124 | tf_op jit(solution)/shard_map/while/body/eval_jaxpr/qhe,khe->hqk/dot_general | solution.py:123
  329.5 12.9 %bitcast_add_fusion.5 = f32[1024,12,64]{0,2,1:T(8,128)} fusion(f32[1024,12,64]{0,2,1:T(8,128)} %get-tuple-element.529, f32[12,512,1024]{2,1,0:T(8,128)} %fusion.130, f32[12,512]{1,0:T(8,128)S(1)} %dynamic-slice_bitcast_fusion.2, pred[1024]{0:T(1024)(128)(4,1)S(1)} %compare_reduce_fusion.5, pred[]{:T(512)S(6)} %compare.3, ...), kind=kOutput, calls=%fused_computation.23.clone.1 | convolution fusion | flops 832045056 | bytes 32277508 | tf_op jit(solution)/shard_map/while/body/eval_jaxpr/hqk,qhe->khe/dot_general | solution.py:155
  342.5 17.7 %multiply_reduce_fusion.5 = (f32[12,512]{1,0:T(8,128)S(1)}, f32[12,512,1024]{2,1,0:T(8,128)}) fusion(f32[12,512,1024]{2,1,0:T(8,128)} %fusion.130, f32[12,512]{1,0:T(8,128)S(1)} %dynamic-slice_bitcast_fusion.2, pred[1024]{0:T(1024)(128)(4,1)S(1)} %compare_reduce_fusion.5, bf16[1024,12,64]{0,2,1:T(8,128)(2,1)} %get-tuple-element.547, ...), kind=kOutput, calls=%fused_computation.18.clone.1 | convolution fusion | flops 836757504 | bytes 52741124 | tf_op jit(solution)/shard_map/while/body/eval_jaxpr/qhe,khe->hqk/dot_general | solution.py:144
  360.2 21.5 %multiply_convert_fusion.3 = bf16[12,512,1024]{2,1,0:T(8,128)(2,1)} fusion(f32[12,512,1024]{2,1,0:T(8,128)} %get-tuple-element.489, f32[12,512,1024]{2,1,0:T(8,128)} %fusion.130, f32[12,512]{1,0:T(8,128)S(1)} %get-tuple-element.490, f32[12,512]{1,0:T(8,128)S(1)} %dynamic-slice_bitcast_fusion.2, pred[1024]{0:T(1024)(128)(4,1)S(1)} %compare_reduce_fusion.5), kind=kLoop, calls=%fused_computation.17.clone.1 | loop fusion | flops 37748736 | bytes 62964736 | tf_op jit(solution)/shard_map/while/body/eval_jaxpr/convert_element_type | solution.py:148
  381.6 9.4 %bitcast_dynamic-update-slice_fusion.8 = bf16[2,512,12,64]{1,3,2,0:T(8,128)(2,1)} fusion(bf16[2,512,12,64]{1,3,2,0:T(8,128)(2,1)} %get-tuple-element.530, s32[]{:T(128)S(6)} %copy.141, bf16[12,512,1024]{2,1,0:T(8,128)(2,1)} %multiply_convert_fusion.3, bf16[1024,12,64]{0,2,1:T(8,128)(2,1)S(1)} %get-tuple-element.544), kind=kOutput, calls=%fused_computation.25.clone.1 | convolution fusion | flops 805699584 | bytes 15728644 | tf_op jit(solution)/shard_map/while/body/eval_jaxpr/hqk,khe->qhe/dot_general | solution.py:149
  391.0 8.6 %bitcast_add_fusion.4 = f32[1024,12,64]{0,2,1:T(8,128)} fusion(f32[1024,12,64]{0,2,1:T(8,128)} %get-tuple-element.528, bf16[12,512,1024]{2,1,0:T(8,128)(2,1)} %multiply_convert_fusion.3, pred[]{:T(512)S(6)} %compare.3, bf16[2,512,12,64]{1,3,2,0:T(8,128)(2,1)S(1)} %get-tuple-element.543, s32[]{:T(128)S(6)} %copy.141), kind=kOutput, calls=%fused_computation.24.clone.1 | convolution fusion | flops 807665664 | bytes 19660804 | tf_op jit(solution)/shard_map/while/body/eval_jaxpr/hqk,qhe->khe/dot_general | solution.py:152
  400.3 10.1 %fusion.130 = f32[12,512,1024]{2,1,0:T(8,128)} fusion(bf16[1024,12,64]{0,2,1:T(8,128)(2,1)S(1)} %get-tuple-element.544, bf16[2,512,12,64]{1,3,2,0:T(8,128)(2,1)S(1)} %get-tuple-element.543, s32[]{:T(128)S(6)} %copy.141), kind=kOutput, calls=%fused_computation.30.clone.1 | convolution fusion | flops 805306368 | bytes 27525124 | tf_op jit(solution)/shard_map/while/body/eval_jaxpr/qhe,khe->hqk/dot_general | solution.py:123
  410.4 13.8 %bitcast_add_fusion.5 = f32[1024,12,64]{0,2,1:T(8,128)} fusion(f32[1024,12,64]{0,2,1:T(8,128)} %get-tuple-element.529, f32[12,512,1024]{2,1,0:T(8,128)} %fusion.130, f32[12,512]{1,0:T(8,128)S(1)} %dynamic-slice_bitcast_fusion.2, pred[1024]{0:T(1024)(128)(4,1)S(1)} %compare_reduce_fusion.5, pred[]{:T(512)S(6)} %compare.3, ...), kind=kOutput, calls=%fused_computation.23.clone.1 | convolution fusion | flops 832045056 | bytes 32277508 | tf_op jit(solution)/shard_map/while/body/eval_jaxpr/hqk,qhe->khe/dot_general | solution.py:155
  424.2 17.4 %multiply_reduce_fusion.5 = (f32[12,512]{1,0:T(8,128)S(1)}, f32[12,512,1024]{2,1,0:T(8,128)}) fusion(f32[12,512,1024]{2,1,0:T(8,128)} %fusion.130, f32[12,512]{1,0:T(8,128)S(1)} %dynamic-slice_bitcast_fusion.2, pred[1024]{0:T(1024)(128)(4,1)S(1)} %compare_reduce_fusion.5, bf16[1024,12,64]{0,2,1:T(8,128)(2,1)} %get-tuple-element.547, ...), kind=kOutput, calls=%fused_computation.18.clone.1 | convolution fusion | flops 836757504 | bytes 52741124 | tf_op jit(solution)/shard_map/while/body/eval_jaxpr/qhe,khe->hqk/dot_general | solution.py:144
  441.7 21.5 %multiply_convert_fusion.3 = bf16[12,512,1024]{2,1,0:T(8,128)(2,1)} fusion(f32[12,512,1024]{2,1,0:T(8,128)} %get-tuple-element.489, f32[12,512,1024]{2,1,0:T(8,128)} %fusion.130, f32[12,512]{1,0:T(8,128)S(1)} %get-tuple-element.490, f32[12,512]{1,0:T(8,128)S(1)} %dynamic-slice_bitcast_fusion.2, pred[1024]{0:T(1024)(128)(4,1)S(1)} %compare_reduce_fusion.5), kind=kLoop, calls=%fused_computation.17.clone.1 | loop fusion | flops 37748736 | bytes 62964736 | tf_op jit(solution)/shard_map/while/body/eval_jaxpr/convert_element_type | solution.py:148
  463.1 9.4 %bitcast_dynamic-update-slice_fusion.8 = bf16[2,512,12,64]{1,3,2,0:T(8,128)(2,1)} fusion(bf16[2,512,12,64]{1,3,2,0:T(8,128)(2,1)} %get-tuple-element.530, s32[]{:T(128)S(6)} %copy.141, bf16[12,512,1024]{2,1,0:T(8,128)(2,1)} %multiply_convert_fusion.3, bf16[1024,12,64]{0,2,1:T(8,128)(2,1)S(1)} %get-tuple-element.544), kind=kOutput, calls=%fused_computation.25.clone.1 | convolution fusion | flops 805699584 | bytes 15728644 | tf_op jit(solution)/shard_map/while/body/eval_jaxpr/hqk,khe->qhe/dot_general | solution.py:149
  472.5 9.5 %bitcast_add_fusion.4 = f32[1024,12,64]{0,2,1:T(8,128)} fusion(f32[1024,12,64]{0,2,1:T(8,128)} %get-tuple-element.528, bf16[12,512,1024]{2,1,0:T(8,128)(2,1)} %multiply_convert_fusion.3, pred[]{:T(512)S(6)} %compare.3, bf16[2,512,12,64]{1,3,2,0:T(8,128)(2,1)S(1)} %get-tuple-element.543, s32[]{:T(128)S(6)} %copy.141), kind=kOutput, calls=%fused_computation.24.clone.1 | convolution fusion | flops 807665664 | bytes 19660804 | tf_op jit(solution)/shard_map/while/body/eval_jaxpr/hqk,qhe->khe/dot_general | solution.py:152
  482.2 3.2 copy.102
  486.1 3.0 convert.14
  490.4 7.0 fusion.63
  498.8 10.2 %fusion.55 = f32[3072,768]{1,0:T(8,128)} fusion(bf16[1024,3072]{1,0:T(8,128)(2,1)} %get-tuple-element.353, bf16[1024,768]{0,1:T(8,128)(2,1)S(1)} %copy-done.12, pred[1024]{0:T(1024)(128)(4,1)S(1)} %copy-done.51), kind=kOutput, calls=%fused_computation.94 | convolution fusion | flops 4834197504 | bytes 17302528 | tf_op jit(solution)/shard_map/dot_general | solution.py:30
  509.7 11.4 %fusion.67 = f32[768,3072]{1,0:T(8,128)} fusion(bf16[1024,3072]{1,0:T(8,128)(2,1)} %get-tuple-element.374, f32[1024,768]{0,1:T(8,128)} %copy-done.7, f32[768]{0:T(1024)S(1)} %copy-done.45, f32[768]{0:T(1024)S(1)} %copy-done.35, f32[1024]{0:T(1024)S(1)} %copy-done.39, f32[1024]{0:T(1024)S(1)} %copy-done.29), kind=kOutput, calls=%fused_computation.113 | convolution fusion | flops 4835770368 | bytes 18888704 | tf_op jit(solution)/shard_map/dot_general | solution.py:30
  525.1 10.2 %select_convert_fusion = bf16[1024,768]{0,1:T(8,128)(2,1)} fusion(f32[1024,768]{0,1:T(8,128)} %copy-done.7, bf16[1024,3072]{1,0:T(8,128)(2,1)} %get-tuple-element.353, bf16[3072,768]{0,1:T(8,128)(2,1)} %all-gather.13.cloned.1.call-done, f32[768]{0:T(1024)S(1)} %convert_element_type.123, pred[1024]{0:T(1024)(128)(4,1)S(1)} %copy-done.51), kind=kOutput, calls=%fused_computation.89 | convolution fusion | flops 4834983936 | bytes 15732736 | tf_op jit(solution)/shard_map/dot_general | solution.py:26
  535.3 2.6 copy.106
  537.9 25.9 %reduce-scatter.15.cloned.1.call-done = f32[96,2304]{1,0:T(8,128)} async-done(((f32[768,2304]{1,0:T(8,128)}), f32[96,2304]{1,0:T(8,128)}) %reduce-scatter.15.cloned.1.call-update) | async-done | bytes 884752 | tf_op jit(solution)/shard_map/reduce_scatter | solution.py:303
  565.8 2.1 copy.110
  568.0 9.1 %fusion.77 = (f32[768]{0:T(1024)S(1)}, f32[1024,768]{1,0:T(8,128)}) fusion(bf16[768,2304]{1,0:T(8,128)(2,1)} %all-gather.7.cloned.1.call-done, bf16[1024,768]{0,1:T(8,128)(2,1)} %bitcast.139, bf16[1024,768]{0,1:T(8,128)(2,1)} %bitcast.136, bf16[1024,768]{0,1:T(8,128)(2,1)} %bitcast.133), kind=kOutput, calls=%fused_computation.121 | convolution fusion | flops 3638820096 | bytes 11406336 | tf_op jit(solution)/shard_map/dot_general | solution.py:36
  577.2 4.2 copy.103
  581.3 62.5 %reduce-scatter.23.cloned.1.call-done = f32[384,768]{1,0:T(8,128)} async-done(((f32[3072,768]{1,0:T(8,128)}), f32[384,768]{1,0:T(8,128)}) %reduce-scatter.23.cloned.1.call-update) | async-done | bytes 1179664 | tf_op jit(solution)/shard_map/reduce_scatter | solution.py:306
  643.8 2.1 convert_element_type.140
  646.0 2.1 copy.114
  648.2 2.9 convert_reduce_fusion.1
  652.1 71.7 %reduce-scatter.19.cloned.1.call-done = f32[96,3072]{1,0:T(8,128)} async-done(((f32[768,3072]{1,0:T(8,128)}), f32[96,3072]{1,0:T(8,128)}) %reduce-scatter.19.cloned.1.call-update) | async-done | bytes 1179664 | tf_op jit(solution)/shard_map/reduce_scatter | solution.py:305
  723.8 2.2 convert_element_type.137
  726.0 3.3 fusion.49
  729.4 4.7 fusion.52
  734.1 24.0 %all-reduce.15 = (f32[1536]{0:T(1024)S(1)}, f32[768]{0:T(1024)S(1)}, f32[3072]{0:T(1024)S(1)}, f32[768]{0:T(1024)S(1)}, f32[768]{0:T(1024)S(1)}, /*index=5*/f32[...) all-reduce(f32[1536]{0:T(1024)S(1)} %pad_maximum_fusion.2, ...), channel_id=4, replica_groups=mesh['dp'=8,'fsdp'=4] {'dp'}, use_global_device_ids=true, to_apply=%region_18.19.clone | all-reduce | flops 9216 | bytes 73728
  758.6 2.6 copy.107
  761.3 12.4 %all-reduce.16 = (f32[192]{0:T(256)}, f32[96]{0:T(128)}, f32[384]{0:T(512)}, f32[96]{0:T(128)}, f32[96]{0:T(128)}, /*index=5*/f32[96]{0:T(128)}, f32[96]{0:T(128)}, f32[96]{0:T(128)}) all-reduce(f32[192]{0:T(256)S(1)} %dynamic-slice.8, f32[96]{0:T(128)S(1)} %dynamic-slice.10, ...), channel_id=1, replica_groups=mesh['dp'=8,'fsdp'=4] {'fsdp'}, use_global_device_ids=true, to_apply=%region_19.20 | all-reduce | flops 1152 | bytes 9216 | tf_op jit(solution)/shard_map/psum | solution.py:330
  777.0 14.4 %reduce-scatter.29.cloned.1.call-done = bf16[192,384]{1,0:T(8,128)(2,1)} async-done(((bf16[768,384]{1,0:T(8,128)(2,1)}), bf16[192,384]{1,0:T(8,128)(2,1)}) %reduce-scatter.29.cloned.1.call-update) | async-done | bytes 147472
  793.3 20.7 %reduce-scatter.21.cloned.1.call-done = bf16[96,768]{1,0:T(8,128)(2,1)} async-done(((bf16[96,3072]{1,0:T(8,128)(2,1)}), bf16[96,768]{1,0:T(8,128)(2,1)}) %reduce-scatter.21.cloned.1.call-update) | async-done | bytes 147472 | tf_op jit(solution)/shard_map/reduce_scatter | solution.py:323
  (253 shorter events, 53.0 us)
Async XLA Ops:
  7.2 34.8 %copy-start.22 = (bf16[96,768]{1,0:T(8,128)(2,1)S(1)}, bf16[96,768]{1,0:T(8,128)(2,1)}, u32[]{:S(2)}) copy-start(bf16[96,768]{1,0:T(8,128)(2,1)} %param.26) | copy-start | bytes 442372
  7.2 52.7 %copy-start.23 = (bf16[384,192]{0,1:T(8,128)(2,1)S(1)}, bf16[384,192]{0,1:T(8,128)(2,1)}, u32[]{:S(2)}) copy-start(bf16[384,192]{0,1:T(8,128)(2,1)} %param.28) | copy-start | bytes 442372
  7.2 112.0 %all-gather.7.cloned.1.call-start = ((), (), s32[]{:S(2)}) async-start(), calls=%async_computation.8 | async-start | bytes 3981312 | tf_op jit(solution)/shard_map/all_gather | solution.py:62
  7.2 69.3 %copy-start.53 = (u32[32]{0:T(128)S(1)}, u32[32]{0:T(128)}, u32[]{:S(2)}) copy-start(u32[32]{0:T(128)} %constant.123) | copy-start | bytes 388
  7.3 71.8 %copy-start.54 = (bf16[384]{0:T(512)(128)(2,1)S(1)}, bf16[384]{0:T(512)(128)(2,1)}, u32[]{:S(2)}) copy-start(bf16[384]{0:T(512)(128)(2,1)} %param.27) | copy-start | bytes 2308
  7.3 71.8 %copy-start.56 = (bf16[96]{0:T(256)(128)(2,1)S(1)}, bf16[96]{0:T(256)(128)(2,1)}, u32[]{:S(2)}) copy-start(bf16[96]{0:T(256)(128)(2,1)} %param.32) | copy-start | bytes 580
  7.3 72.0 %copy-start.57 = (bf16[96]{0:T(256)(128)(2,1)S(1)}, bf16[96]{0:T(256)(128)(2,1)}, u32[]{:S(2)}) copy-start(bf16[96]{0:T(256)(128)(2,1)} %param.33) | copy-start | bytes 580
  7.3 72.2 %copy-start.58 = (bf16[96]{0:T(256)(128)(2,1)S(1)}, bf16[96]{0:T(256)(128)(2,1)}, u32[]{:S(2)}) copy-start(bf16[96]{0:T(256)(128)(2,1)} %param.25) | copy-start | bytes 580
  7.3 72.5 %copy-start.59 = (bf16[96]{0:T(256)(128)(2,1)S(1)}, bf16[96]{0:T(256)(128)(2,1)}, u32[]{:S(2)}) copy-start(bf16[96]{0:T(256)(128)(2,1)} %param.30) | copy-start | bytes 580
  7.3 72.7 %copy-start.60 = (bf16[96]{0:T(256)(128)(2,1)S(1)}, bf16[96]{0:T(256)(128)(2,1)}, u32[]{:S(2)}) copy-start(bf16[96]{0:T(256)(128)(2,1)} %param.31) | copy-start | bytes 580
  7.3 72.9 %copy-start.61 = (bf16[96]{0:T(256)(128)(2,1)S(1)}, bf16[96]{0:T(256)(128)(2,1)}, u32[]{:S(2)}) copy-start(bf16[96]{0:T(256)(128)(2,1)} %param.29) | copy-start | bytes 580
  7.3 73.1 %copy-start.62 = (bf16[192]{0:T(256)(128)(2,1)S(1)}, bf16[192]{0:T(256)(128)(2,1)}, u32[]{:S(2)}) copy-start(bf16[192]{0:T(256)(128)(2,1)} %param.23) | copy-start | bytes 1156
  24.7 90.1 %copy-start.18 = (bf16[1024,768]{1,0:T(8,128)(2,1)S(1)}, bf16[1024,768]{1,0:T(8,128)(2,1)}, u32[]{:S(2)}) copy-start(bf16[1024,768]{1,0:T(8,128)(2,1)} %param.19) | copy-start | bytes 4718596
  26.1 188.1 %all-gather.9.cloned.1.call-start = ((), (), s32[]{:S(2)}) async-start(), calls=%async_computation.9 | async-start | bytes 1327104 | tf_op jit(solution)/shard_map/all_gather | solution.py:63
  41.9 178.4 %all-gather.11.cloned.1.call-start = ((), (), s32[]{:S(2)}) async-start(), calls=%async_computation.10 | async-start | bytes 5308416 | tf_op jit(solution)/shard_map/all_gather | solution.py:64
  59.8 198.3 %all-gather.13.cloned.1.call-start = ((), (), s32[]{:S(2)}) async-start(), calls=%async_computation.11 | async-start | bytes 5308416 | tf_op jit(solution)/shard_map/all_gather | solution.py:65
  75.8 447.4 %reduce-scatter.17.cloned.1.call-start = ((), (), s32[]{:S(2)}) async-start(), calls=%async_computation.13 | async-start | bytes 2654208 | tf_op jit(solution)/shard_map/reduce_scatter | solution.py:304
  103.9 15.3 %copy-start.26 = (f32[768]{0:T(1024)}, f32[768]{0:T(1024)S(1)}, u32[]{:S(2)}) copy-start(f32[768]{0:T(1024)S(1)} %convert_element_type.110) | copy-start | bytes 9220
  104.5 14.7 %copy-start.46 = (f32[768]{0:T(1024)}, f32[768]{0:T(1024)S(1)}, u32[]{:S(2)}) copy-start(f32[768]{0:T(1024)S(1)} %convert_element_type.111) | copy-start | bytes 9220
  115.6 3.7 copy-start.2
  115.6 2.0 copy-start.19
  115.9 9.8 %copy-start.24 = (f32[1024]{0:T(1024)}, f32[1024]{0:T(1024)S(1)}, u32[]{:S(2)}) copy-start(f32[1024]{0:T(1024)S(1)} %broadcast_multiply_fusion.1) | copy-start | bytes 12292
  116.3 9.4 %copy-start.32 = (f32[1024]{0:T(1024)}, f32[1024]{0:T(1024)S(1)}, u32[]{:S(2)}) copy-start(f32[1024]{0:T(1024)S(1)} %fusion.50) | copy-start | bytes 12292
  117.6 8.1 copy-start.30
  149.9 12.0 %copy-start.1 = (bf16[1024,12,64]{0,2,1:T(8,128)(2,1)S(1)}, bf16[1024,12,64]{0,2,1:T(8,128)(2,1)}, u32[]{:S(2)}) copy-start(bf16[1024,12,64]{0,2,1:T(8,128)(2,1)} %get-tuple-element.512) | copy-start | bytes 4718596 | tf_op jit(solution)/shard_map/while
  149.9 12.1 %copy-start.13 = (bf16[2,512,12,64]{1,3,2,0:T(8,128)(2,1)S(1)}, bf16[2,512,12,64]{1,3,2,0:T(8,128)(2,1)}, u32[]{:S(2)}) copy-start(bf16[2,512,12,64]{1,3,2,0:T(8,128)(2,1)} %get-tuple-element.500) | copy-start | bytes 4718596 | tf_op jit(solution)/shard_map/while
  185.5 11.4 %copy-start.1 = (bf16[1024,12,64]{0,2,1:T(8,128)(2,1)S(1)}, bf16[1024,12,64]{0,2,1:T(8,128)(2,1)}, u32[]{:S(2)}) copy-start(bf16[1024,12,64]{0,2,1:T(8,128)(2,1)} %get-tuple-element.512) | copy-start | bytes 4718596 | tf_op jit(solution)/shard_map/while
  185.5 11.4 %copy-start.13 = (bf16[2,512,12,64]{1,3,2,0:T(8,128)(2,1)S(1)}, bf16[2,512,12,64]{1,3,2,0:T(8,128)(2,1)}, u32[]{:S(2)}) copy-start(bf16[2,512,12,64]{1,3,2,0:T(8,128)(2,1)} %get-tuple-element.500) | copy-start | bytes 4718596 | tf_op jit(solution)/shard_map/while
  209.6 4.6 copy-start.48
  218.2 2.1 copy-start.34
  218.2 2.1 copy-start.42
  218.2 2.1 copy-start.44
  218.2 77.3 %copy-start.28 = (f32[1024]{0:T(1024)}, f32[1024]{0:T(1024)S(1)}, u32[]{:S(2)}) copy-start(f32[1024]{0:T(1024)S(1)} %broadcast_multiply_fusion) | copy-start | bytes 12292
  220.3 75.2 %copy-start.38 = (f32[1024]{0:T(1024)}, f32[1024]{0:T(1024)S(1)}, u32[]{:S(2)}) copy-start(f32[1024]{0:T(1024)S(1)} %fusion.60) | copy-start | bytes 12292
  220.3 37.8 %copy-start.50 = (pred[1024]{0:T(1024)(128)(4,1)S(1)}, pred[1024]{0:T(1024)(128)(4,1)}, u32[]{:S(2)}) copy-start(pred[1024]{0:T(1024)(128)(4,1)} %iota_compare_fusion) | copy-start | bytes 3076
  258.1 20.3 %copy-start.55 = (bf16[768,3072]{1,0:T(8,128)(2,1)S(1)}, bf16[768,3072]{1,0:T(8,128)(2,1)}, u32[]{:S(2)}) copy-start(bf16[768,3072]{1,0:T(8,128)(2,1)} %all-gather.11.cloned.1.call-done) | copy-start | bytes 14155780
  291.0 4.5 copy-start.8
  291.0 4.7 copy-start.9
  297.1 2.4 copy-start.20
  316.0 247.8 %reduce-scatter.15.cloned.1.call-start = ((), (), s32[]{:S(2)}) async-start(), calls=%async_computation.12 | async-start | bytes 7962624 | tf_op jit(solution)/shard_map/reduce_scatter | solution.py:303
  318.5 11.1 %copy-start.10 = (bf16[2,512,12,64]{1,3,2,0:T(8,128)(2,1)S(1)}, bf16[2,512,12,64]{1,3,2,0:T(8,128)(2,1)}, u32[]{:S(2)}) copy-start(bf16[2,512,12,64]{1,3,2,0:T(8,128)(2,1)} %get-tuple-element.546) | copy-start | bytes 4718596 | tf_op jit(solution)/shard_map/while
  400.3 10.1 %copy-start.10 = (bf16[2,512,12,64]{1,3,2,0:T(8,128)(2,1)S(1)}, bf16[2,512,12,64]{1,3,2,0:T(8,128)(2,1)}, u32[]{:S(2)}) copy-start(bf16[2,512,12,64]{1,3,2,0:T(8,128)(2,1)} %get-tuple-element.546) | copy-start | bytes 4718596 | tf_op jit(solution)/shard_map/while
  482.2 3.6 copy-start
  485.8 3.4 copy-start.15
  486.0 3.1 copy-start.16
  486.0 4.3 copy-start.3
  486.1 4.3 copy-start.25
  486.1 4.3 copy-start.27
  486.1 4.3 copy-start.31
  486.1 4.3 copy-start.47
  497.4 146.4 %reduce-scatter.23.cloned.1.call-start = ((), (), s32[]{:S(2)}) async-start(), calls=%async_computation.16 | async-start | bytes 10616832 | tf_op jit(solution)/shard_map/reduce_scatter | solution.py:306
  509.1 214.8 %reduce-scatter.19.cloned.1.call-start = ((), (), s32[]{:S(2)}) async-start(), calls=%async_computation.14 | async-start | bytes 10616832 | tf_op jit(solution)/shard_map/reduce_scatter | solution.py:305
  521.2 2.0 copy-start.52
  521.2 252.5 %reduce-scatter.27.cloned.1.call-start = ((), (), s32[]{:S(2)}) async-start(), calls=%async_computation.18 | async-start | bytes 245760
  525.1 250.1 %reduce-scatter.25.cloned.1.call-start = ((), (), s32[]{:S(2)}) async-start(), calls=%async_computation.17 | async-start | bytes 737280
  568.0 223.4 %reduce-scatter.29.cloned.1.call-start = ((), (), s32[]{:S(2)}) async-start(), calls=%async_computation.19 | async-start | bytes 737280
  648.1 165.9 %reduce-scatter.21.cloned.1.call-start = ((), (), s32[]{:S(2)}) async-start(), calls=%async_computation.15 | async-start | bytes 737280 | tf_op jit(solution)/shard_map/reduce_scatter | solution.py:323
  648.2 3.3 copy-start.4
  652.1 77.3 %copy-start.37 = (f32[1024]{0:T(1024)S(1)}, f32[1024]{0:T(1024)}, u32[]{:S(2)}) copy-start(f32[1024]{0:T(1024)} %copy-done.36) | copy-start | bytes 12292
  726.0 3.3 copy-start.5
  729.4 4.8 copy-start.40
  729.4 4.8 copy-start.41
  729.4 4.7 copy-start.43
  729.4 4.7 copy-start.49
  (15 other events, 18.1 us)
Sparse Core Ops, SparseCore 0:
  26.2 35.7 all-gather.6
  64.5 24.1 all-gather.8
  90.6 38.9 all-gather.10
  131.3 39.7 all-gather.12
  316.2 43.1 reduce-scatter.16
  497.6 66.2 reduce-scatter.14
  567.3 76.4 reduce-scatter.22
  647.3 76.4 reduce-scatter.18
  726.7 19.3 reduce-scatter.26
  748.3 20.2 reduce-scatter.24
  771.0 20.3 reduce-scatter.28
  793.6 20.3 reduce-scatter.20
where the time goes:
time: 828 us; the launch traced here: 823 us
  matrix products  295 us (36%)
  waiting for transfers between devices  195 us (24%)
  blocking collectives  133 us (16%)
  other arithmetic  105 us (13%)
  local copies, waits for them, and re-layouts  73.2 us (9%)
  between operations  19.2 us (2%)
    reduce_scatter x1, waiting for transfers between devices, per_device(): lax.psum_scatter(grad_expand, 'dp', scatter_dimension=0, tiled=True)  71.7 us
    reduce_scatter x1, waiting for transfers between devices, per_device(): lax.psum_scatter(grad_contract, 'dp', scatter_dimension=0, tiled=True)  62.5 us
    dot_general x4, matrix products, matmul(): return jnp.dot(first, second, preferred_element_type=jnp.float32)  58.2 us
    unnamed x2, blocking collectives  47.2 us
    convert_element_type x2, other arithmetic, attend_backward(): grad_scores = (weights * (grad_weights - row_inner)).astype(jnp.bfloat16)  42.9 us
    dot_general x4, matrix products, over_columns(): lax.dot_general(first, second, (((1,), (1,)), ((), ())), preferred_elemen...  42.7 us
    dot_general x4, matrix products, block_scores(): jnp.einsum('qhe,khe->hqk', query_block, keys_all, preferred_element_type=...  41.5 us
    unnamed x159, local copies, waits for them, and re-layouts  36.5 us
  transfers between devices with their start and end apart: 12, of which 5 were waited for; matrix products, arithmetic and copies ran while one was open for 49% of the time, Pallas kernels for 0%

commit v1 on v0

--- a/solution.py
+++ b/solution.py
@@ -1,14 +1,401 @@
+import functools
 import jax
 import jax.numpy as jnp
 from jax import lax
+from jax.experimental import pallas as pl
+from jax.experimental.pallas import tpu as pltpu
 from jax.sharding import PartitionSpec as P
 
 H = 12
 HD = 64
-
-
+F32 = jnp.float32
+BF = jnp.bfloat16
+MESH = pl.DeviceIdType.MESH
 eps_norm = 1e-05
 neg_fill = -1000000000.0
+
+
+def dot(first, second):
+    return jnp.dot(first, second, preferred_element_type=F32)
+
+
+def dot_nt(first, second):
+    return lax.dot_general(first, second, (((1,), (1,)), ((), ())), preferred_element_type=F32)
+
+
+def dot_tn(first, second):
+    return lax.dot_general(first, second, (((0,), (0,)), ((), ())), preferred_element_type=F32)
+
+
+def mo(value, multiple):
+    return pl.multiple_of(value, multiple)
+
+
+class Place:
+    def __init__(self):
+        self.d = lax.axis_index("dp")
+        self.z = lax.axis_index("fsdp")
+        core = lax.rem(self.d, 2)
+        across = lax.rem(lax.div(self.d, 2), 2)
+        up = lax.div(self.d, 4)
+        self.dc = self.d + 1 - 2 * core
+        self.dx = self.d + 2 - 4 * across
+        self.dy = self.d + 4 - 8 * up
+        self.dd = self.dx + 4 - 8 * up
+        self.odd = lax.rem(self.z, 2)
+
+    def zt(self, step):
+        return lax.rem(self.z + step, 4)
+
+    def zf(self, step):
+        return lax.rem(self.z + 4 - step, 4)
+
+    def id(self, to):
+        if to == "x":
+            return (self.dx, self.z)
+        if to == "y":
+            return (self.dy, self.z)
+        if to == "c":
+            return (self.dc, self.z)
+        return (self.d, self.zt(to))
+
+
+def enter(place):
+    barrier = pltpu.get_barrier_semaphore()
+    for to in ("x", "y", "c", 1, 2, 3):
+        pl.semaphore_signal(barrier, inc=1, device_id=place.id(to), device_id_type=MESH)
+    pl.semaphore_wait(barrier, 6)
+
+
+class Link:
+    def __init__(self, place, send_sem, recv_sem):
+        self.place, self.send_sem, self.recv_sem = place, send_sem, recv_sem
+        self.count = 0
+        self.copies = []
+
+    def slot(self):
+        self.count += 1
+        return self.count - 1
+
+    def copy(self, slot, source, target, to):
+        return pltpu.make_async_remote_copy(
+            src_ref=source, dst_ref=target, send_sem=self.send_sem.at[slot],
+            recv_sem=self.recv_sem.at[slot], device_id=self.place.id(to), device_id_type=MESH)
+
+    def send(self, slot, source, target, to, like):
+        self.copy(slot, source, target, to).start()
+        self.copies.append((slot, like))
+
+    def got(self, slot, target):
+        self.copy(slot, target, target, "x").wait_recv()
+
+    def finish(self):
+        for slot, like in self.copies:
+            view = like()
+            self.copy(slot, view, view, "x").wait_send()
+
+
+def gather_events(link, place, block):
+    p = place
+    zs = [link.slot() for _ in range(4)]
+    xs = [link.slot() for _ in range(4)]
+    ys = [link.slot() for _ in range(4)]
+    fx = [link.slot() for _ in range(4)]
+    cs = [[link.slot() for _ in range(4)] for _ in range(4)]
+    got = link.got
+    send = functools.partial(link.send, like=lambda: block(0, 0))
+
+    def begin():
+        own = block(p.z, p.d)
+        for step in (1, 3, 2):
+            send(zs[step], own, own, step)
+        for slots, to in ((xs, "x"), (ys, "y")):
+            send(slots[0], own, own, to)
+        send(cs[0][0], own, own, "c")
+
+    def onward(step):
+        def run():
+            here = block(p.zf(step), p.d)
+            got(zs[step], here)
+            for slots, to in ((xs, "x"), (ys, "y")):
+                send(slots[step], here, here, to)
+            send(cs[0][step], here, here, "c")
+        return run
+
+    def turn(step):
+        def run():
+            z = p.zf(step)
+            bx, by = block(z, p.dx), block(z, p.dy)
+            got(xs[step], bx)
+            got(ys[step], by)
+            if step in (0, 1):
+                send(fx[step], bx, bx, "y")
+            else:
+                send(fx[step], by, by, "x")
+            send(cs[1][step], bx, bx, "c")
+            send(cs[2][step], by, by, "c")
+        return run
+
+    def corner(step):
+        def run():
+            z = p.zf(step)
+            bd = block(z, p.dd)
+            got(fx[step], bd)
+            send(cs[3][step], bd, bd, "c")
+        return run
+
+    def close():
+        dc = p.dc
+        core = lax.rem(dc, 2)
+        across = lax.rem(lax.div(dc, 2), 2)
+        up = lax.div(dc, 4)
+        cx = dc + 2 - 4 * across
+        cy = dc + 4 - 8 * up
+        cd = cx + 4 - 8 * up
+        for which, d in enumerate((dc, cx, cy, cd)):
+            for step in range(4):
+                got(cs[which][step], block(p.zf(step), d))
+
+    return ([begin, onward(1), onward(3), turn(0), onward(2), turn(1), turn(3), turn(2)]
+            + [corner(0), corner(1), corner(3), corner(2), close])
+
+
+def window(value, odd, wide):
+    rows, k = value.shape
+    fill = jnp.zeros((rows, wide - k), F32)
+    value = value.astype(F32)
+    left = jnp.concatenate([value, fill], axis=1)
+    right = jnp.concatenate([fill, value], axis=1)
+    return jnp.where(odd == 0, left, right).astype(BF)
+
+
+def merge_windows(blocks, full, tiles, rows_step):
+    rows = full.shape[0]
+    half = tiles // 2
+
+    def body(i, _):
+        r = pl.ds(mo(i * rows_step, rows_step), rows_step)
+        for pair in range(2):
+            even, odd = blocks.at[2 * pair], blocks.at[2 * pair + 1]
+            base = pair * tiles * 128
+            full[r, base:base + half * 128] = even[r, 0:half * 128]
+            full[r, base + half * 128:base + (half + 1) * 128] = (
+                even[r, half * 128:(half + 1) * 128] + odd[r, 0:128])
+            full[r, base + (half + 1) * 128:base + tiles * 128] = odd[r, 128:(half + 1) * 128]
+        return 0
+
+    lax.fori_loop(0, rows // rows_step, body, 0)
+
+
+def split3(value):
+    high = value.astype(BF)
+    rest = value - high.astype(F32)
+    mid = rest.astype(BF)
+    low = (rest - mid.astype(F32)).astype(BF)
+    return high.astype(F32), mid.astype(F32), low.astype(F32)
+
+
+def extend(head, pair, lane, one, two, three, four):
+    base = 64 * (1 - head)
+    extra = jnp.where(lane == base, one, jnp.where(lane == base + 1, two, jnp.where(
+        lane == base + 2, three, jnp.where(lane == base + 3, four, 0.0))))
+    keep = (lane < 64) if head == 0 else (lane >= 64)
+    return jnp.where(keep, pair, extra).astype(BF)
+
+
+def iota(shape, axis):
+    return lax.broadcasted_iota(jnp.int32, shape, axis)
+
+
+QB = 512
+
+
+def first_kernel(length_ref, x_ref, wp_ref, wo_ref, we_ref, vec_ref,
+                 n1_out, proj_out, mixed_out, qa_out, wp_out, wo_out, we_out, v_out,
+                 wp_blk, wo_blk, we, wp, wo, vb, n1, proj, mixed, qa, ka, va, vrow,
+                 send_sem, recv_sem, out_sem):
+    p = Place()
+    T, D = x_ref.shape
+    R = wp_ref.shape[0]
+    FF = we.shape[1]
+    link = Link(p, send_sem, recv_sem)
+    rows_of = lambda d: pl.ds(mo(d * R, 16), R)
+    bp = lambda z, d: wp_blk.at[z, rows_of(d), :]
+    bo = lambda z, d: wo_blk.at[z, rows_of(d), :]
+    be = lambda z, d: we.at[rows_of(d), pl.ds(mo(z * (FF // 4), 128), FF // 4)]
+    ev_p, ev_o, ev_e = (gather_events(link, p, b) for b in (bp, bo, be))
+    vs = [link.slot() for _ in range(7)]
+
+    wp_blk[p.z, rows_of(p.d), :] = window(wp_ref[...], p.odd, wp_blk.shape[2])
+    wo_blk[p.z, rows_of(p.d), :] = window(wo_ref[...], p.odd, wo_blk.shape[2])
+    we[rows_of(p.d), pl.ds(mo(p.z * (FF // 4), 128), FF // 4)] = we_ref[...]
+    vb[p.d] = vec_ref[...]
+
+    outs = []
+
+    def out(source, target):
+        made = pltpu.make_async_copy(source, target, out_sem.at[len(outs)])
+        made.start()
+        outs.append(made)
+
+    enter(p)
+    send_v = lambda slot, d, to: link.send(vs[slot], vb.at[d], vb.at[d], to, lambda: vb.at[0])
+    for slot, to in ((0, "x"), (1, "y"), (3, "c")):
+        send_v(slot, p.d, to)
+    ev_p[0]()
+    link.got(vs[0], vb.at[p.dx])
+    link.got(vs[1], vb.at[p.dy])
+    send_v(2, p.dx, "y")
+    send_v(4, p.dx, "c")
+    send_v(5, p.dy, "c")
+    ev_p[1]()
+    ev_p[2]()
+    link.got(vs[2], vb.at[p.dd])
+    send_v(6, p.dd, "c")
+    ev_p[3]()
+    ev_p[4]()
+    dc = p.dc
+    link.got(vs[3], vb.at[dc])
+    cx = p.dx + p.dc - p.d
+    cy = p.dy + p.dc - p.d
+    cd = p.dd + p.dc - p.d
+    link.got(vs[4], vb.at[cx])
+    link.got(vs[5], vb.at[cy])
+    link.got(vs[6], vb.at[cd])
+    got = vb[...].astype(F32)
+    side = lambda row, wide: jnp.concatenate([got[i, row:row + 1, 0:wide] for i in range(8)], axis=1)
+    bias = side(0, 2 * R)
+    vrow[0:1, 0:D] = bias[:, 0:D]
+    vrow[0:1, D:2 * D] = jnp.zeros((1, D), F32)
+    vrow[0:1, 2 * D:3 * D] = bias[:, D:]
+    vrow[1:2, :] = side(2, FF // 8)
+    for row, at in ((2, 1), (3, 3), (4, 4), (5, 5), (6, 6), (7, 7)):
+        vrow[row:row + 1, 0:D] = side(at, R)
+    out(vrow, v_out)
+    ev_p[5]()
+
+    LR = 128
+    gain, shift = vrow[4:5, 0:D], vrow[5:6, 0:D]
+
+    def norm_body(i, _):
+        r = pl.ds(mo(i * LR, LR), LR)
+        value = x_ref[r, :].astype(F32)
+        u = value - jnp.mean(value, axis=-1, keepdims=True)
+        spread = jnp.mean(u * u, axis=-1, keepdims=True)
+        n1[r, :] = (u * lax.rsqrt(spread + eps_norm) * gain + shift).astype(BF)
+        return 0
+
+    lax.fori_loop(0, T // LR, norm_body, 0)
+    out(n1, n1_out)
+    for event in ev_p[6:]:
+        event()
+    ev_o[0]()
+    merge_windows(wp_blk, wp, 9, 96)
+    out(wp, wp_out)
+    ev_o[1]()
+    ev_o[2]()
+
+    def project_body(i, _):
+        r = pl.ds(mo(i * 256, 256), 256)
+        left = n1[r, :]
+        for j in range(3):
+            cols = slice(j * D, (j + 1) * D)
+            value = dot(left, wp[:, cols]) + vrow[0:1, cols]
+            proj[r, cols] = value.astype(BF)
+        return 0
+
+    lax.fori_loop(0, T // 256, project_body, 0)
+    out(proj, proj_out)
+
+    length = length_ref[0]
+    nq = T // QB
+
+    def attend_steps(events):
+        def body(step, _):
+            for at, event in events:
+                pl.when(step == at)(event)
+            pair = lax.div(step, nq)
+            part = lax.rem(step, nq)
+            cols = lambda off: pl.ds(mo(off + pair * 128, 128), 128)
+
+            @pl.when(part == 0)
+            def _():
+                lane, row = iota((T, 128), 1), iota((T, 128), 0)
+                q = proj[:, cols(0)].astype(F32) * (HD ** -0.5)
+                k = proj[:, cols(D)].astype(F32)
+                v = proj[:, cols(2 * D)].astype(F32)
+                dead = jnp.where(row < length, 0.0, neg_fill)
+                for head in range(2):
+                    ka[head] = extend(head, k, lane, 1.0, 1.0, 1.0, dead)
+                    qa[pair * 2 + head] = extend(head, q, lane, 0.0, 0.0, 0.0, 1.0)
+                    keep = (lane < 64) if head == 0 else (lane >= 64)
+                    va[head] = jnp.where(keep, v, 1.0).astype(BF)
+
+            r = pl.ds(mo(part * QB, QB), QB)
+            lane = iota((QB, 128), 1)
+            halves = []
+            for head in range(2):
+                query = qa[pair * 2 + head, r, :]
+                scores = dot_nt(query, ka[head])
+                top = jnp.max(scores, axis=-1, keepdims=True)
+                powers = jnp.exp(scores - top).astype(BF)
+                value = dot(powers, va[head])
+                total = value[:, 64:65] if head == 0 else value[:, 0:1]
+                one, two, three = split3(-(top + jnp.log(total)))
+                qa[pair * 2 + head, r, :] = extend(head, query.astype(F32), lane, one, two, three, 1.0)
+                halves.append(value * (1.0 / total))
+            mixed[r, cols(0)] = jnp.where(lane < 64, halves[0], halves[1]).astype(BF)
+            return 0
+
+        lax.fori_loop(0, (H // 2) * nq, body, 0)
+
+    rest = ev_o[3:] + ev_e
+    spots = [0, 0, 0, 0, 1, 1, 1, 1, 1, 1] + [2, 3, 3, 4, 4, 5, 5, 6, 7, 8, 8, 9, 10]
+    assert len(rest) == len(spots)
+    attend_steps(list(zip(spots, rest)))
+    merge_windows(wo_blk, wo, 3, 96)
+    out(wo, wo_out)
+    out(we, we_out)
+    out(mixed, mixed_out)
+    out(qa, qa_out)
+    link.finish()
+    for made in outs:
+        made.wait()
+
+
+def first_call(length, x, wp, wo, we, vec):
+    T, D = x.shape
+    FF = we.shape[1] * 4
+    ANY = pl.BlockSpec(memory_space=pl.ANY)
+    V = pl.BlockSpec(memory_space=pltpu.VMEM)
+    S = pl.BlockSpec(memory_space=pltpu.SMEM)
+    sds = jax.ShapeDtypeStruct
+    n = 3 * 32 + 7
+    return pl.pallas_call(
+        first_kernel,
+        in_specs=[S, V, V, V, V, V],
+        out_specs=[ANY] * 8,
+        out_shape=[sds((T, D), BF), sds((T, 3 * D), BF), sds((T, D), BF), sds((H, T, 128), BF),
+                   sds((D, 3 * D), BF), sds((D, D), BF), sds((D, FF), BF), sds((8, FF), F32)],
+        scratch_shapes=[
+            pltpu.VMEM((4, D, 640), BF), pltpu.VMEM((4, D, 256), BF), pltpu.VMEM((D, FF), BF),
+            pltpu.VMEM((D, 3 * D), BF), pltpu.VMEM((D, D), BF), pltpu.VMEM((8,) + vec.shape, BF),
+            pltpu.VMEM((T, D), BF), pltpu.VMEM((T, 3 * D), BF), pltpu.VMEM((T, D), BF),
+            pltpu.VMEM((H, T, 128), BF), pltpu.VMEM((2, T, 128), BF), pltpu.VMEM((2, T, 128), BF),
+            pltpu.VMEM((8, FF), F32),
+            pltpu.SemaphoreType.DMA((n,)), pltpu.SemaphoreType.DMA((n,)), pltpu.SemaphoreType.DMA((8,)),
+        ],
+        compiler_params=pltpu.CompilerParams(
+            collective_id=0, has_side_effects=True, vmem_limit_bytes=60 << 20),
+        name="first_part",
+    )(length, x, wp, wo, we, vec)
+
+
+def pack_vectors(project_bias, output_bias, expand_bias, contract_bias, g1, s1, g2, s2):
+    wide = expand_bias.shape[0]
+    rows = [jnp.pad(v, (0, wide - v.shape[0])) for v in
+            (project_bias, output_bias, expand_bias, contract_bias, g1, s1, g2, s2)]
+    return jnp.pad(jnp.stack(rows), ((0, 8), (0, 0)))
 
 
 def layer_norm(values, gain_row, shift_row):
@@ -358,43 +745,135 @@
     )
 
 
+def back_kernel(length_ref, proj_ref, mixed_ref, qa_ref, dm_ref, dproj_ref, ka_ref, da_ref, dq_ref, va_ref, kT_ref):
+    length = length_ref[0]
+    T, D = mixed_ref.shape
+    KB = 256
+
+    def pair_body(p, _):
+        lane, row = iota((T, 128), 1), iota((T, 128), 0)
+        ps = lambda off: pl.ds(mo(off + p * 128, 128), 128)
+        k = proj_ref[:, ps(D)].astype(F32)
+        v = proj_ref[:, ps(2 * D)].astype(F32)
+        do = dm_ref[:, ps(0)].astype(F32)
+        pr = do * mixed_ref[:, ps(0)].astype(F32)
+        dead = jnp.where(row < length, 0.0, neg_fill)
+        for head in range(2):
+            keep = (lane < 64) if head == 0 else (lane >= 64)
+            delta = jnp.sum(jnp.where(keep, pr, 0.0), axis=-1, keepdims=True)
+            one, two, three = split3(-delta)
+            da_ref[head] = extend(head, do, lane, one, two, three, 0.0)
+            ka_ref[head] = extend(head, k, lane, 1.0, 1.0, 1.0, dead)
+            va_ref[head] = extend(head, v, lane, 1.0, 1.0, 1.0, 0.0)
+            kT_ref[head] = jnp.where(keep, k, 0.0).astype(BF).T
+        dq_ref[...] = jnp.zeros_like(dq_ref)
+
+        def kblk(i, _):
+            rows = pl.ds(mo(i * KB, KB), KB)
+            lk = iota((KB, 128), 1)
+            dks, dvs = [], []
+            for head in range(2):
+                weights = jnp.exp(dot_nt(ka_ref[head, rows, :], qa_ref[p * 2 + head]))
+                low = weights.astype(BF)
+                ds = (weights * dot_nt(va_ref[head, rows, :], da_ref[head])).astype(BF)
+                dvs.append(dot(low, da_ref[head]))
+                dks.append(dot(ds, qa_ref[p * 2 + head]))
+                dq_ref[head] += dot(kT_ref[head, :, rows], ds)
+            dproj_ref[rows, ps(D)] = jnp.where(lk < 64, dks[0], dks[1]).astype(BF)
+            dproj_ref[rows, ps(2 * D)] = jnp.where(lk < 64, dvs[0], dvs[1]).astype(BF)
+            return 0
+
+        lax.fori_loop(0, T // KB, kblk, 0)
+        dproj_ref[:, ps(0)] = ((dq_ref[0] + dq_ref[1]) * (HD ** -0.5)).T.astype(BF)
+        return 0
+
+    lax.fori_loop(0, H // 2, pair_body, 0)
+
+
+def back_call(length, proj, mixed, qa, dm):
+    T, D = mixed.shape
+    V = pl.BlockSpec(memory_space=pltpu.VMEM)
+    return pl.pallas_call(
+        back_kernel, in_specs=[pl.BlockSpec(memory_space=pltpu.SMEM), V, V, V, V], out_specs=V,
+        out_shape=jax.ShapeDtypeStruct((T, 3 * D), BF),
+        scratch_shapes=[pltpu.VMEM((2, T, 128), BF), pltpu.VMEM((2, T, 128), BF), pltpu.VMEM((2, 128, T), F32),
+                        pltpu.VMEM((2, T, 128), BF), pltpu.VMEM((2, 128, T), BF)],
+        compiler_params=pltpu.CompilerParams(vmem_limit_bytes=60 << 20), name="back_part")(
+            length, proj, mixed, qa, dm)
+
+
+def per_device_fast(tokens, lengths, cotangent, project_weight, project_bias, output_weight, output_bias,
+                    expand_weight, expand_bias, contract_weight, contract_bias, first_gain, first_shift,
+                    second_gain, second_shift):
+    T, D = tokens.shape
+    wide = lax.all_gather(contract_weight, "fsdp", axis=1, tiled=True)
+    full_contract = lax.all_gather(wide, "dp", axis=0, tiled=True)
+    vec = pack_vectors(project_bias, output_bias, expand_bias, contract_bias,
+                       first_gain, first_shift, second_gain, second_shift)
+    normed_one, projected, mixed_low, qa, full_project, full_output, full_expand, v = first_call(
+        lengths, tokens, project_weight, output_weight, expand_weight, vec)
+    bias_expand = v[1]
+    bias_output, bias_contract, gain_one, shift_one, gain_two, shift_two = [v[i, :D] for i in range(2, 8)]
+    live = (jnp.arange(T) < lengths[0])[:, None]
+    rows_in = tokens.astype(F32)
+    middle = rows_in + (matmul(mixed_low, full_output) + bias_output)
+    normed_two = layer_norm(middle, gain_two, shift_two).astype(BF)
+    hidden = matmul(normed_two, full_expand) + bias_expand
+    active = gelu_exact(hidden).astype(BF)
+    result = middle + (matmul(active, full_contract) + bias_contract)
+    block_out = jnp.where(live, result, 0.0).astype(BF)
+    grad_out = jnp.where(live, cotangent.astype(F32), 0.0)
+    grad_out_low = grad_out.astype(BF)
+    grad_contract = over_rows(active, grad_out_low)
+    grad_contract_bias = jnp.sum(grad_out, axis=0)
+    grad_active = over_columns(grad_out_low, full_contract)
+    gelu_value, gelu_pull = jax.vjp(gelu_exact, hidden)
+    grad_hidden = gelu_pull(grad_active)[0].astype(BF)
+    grad_expand = over_rows(normed_two, grad_hidden)
+    grad_expand_bias = jnp.sum(grad_hidden.astype(F32), axis=0)
+    grad_normed_two = over_columns(grad_hidden, full_expand)
+    norm_value, second_pull = jax.vjp(layer_norm, middle, gain_two, shift_two)
+    grad_middle, grad_gain_two, grad_shift_two = second_pull(grad_normed_two)
+    grad_middle = grad_middle + grad_out
+    grad_branch = grad_middle.astype(BF)
+    grad_output = over_rows(mixed_low, grad_branch)
+    grad_output_bias = jnp.sum(grad_branch.astype(F32), axis=0)
+    grad_mixed = over_columns(grad_branch, full_output).astype(BF)
+    grad_projected = back_call(lengths, projected, mixed_low, qa, grad_mixed)
+    grad_project = over_rows(normed_one, grad_projected)
+    column_sums = jnp.sum(grad_projected.astype(F32), axis=0)
+    grad_project_bias = jnp.concatenate([column_sums[:D], column_sums[2 * D:]])
+    grad_normed_one = over_columns(grad_projected, full_project)
+    first_value, first_pull = jax.vjp(layer_norm, rows_in, gain_one, shift_one)
+    grad_rows_in, grad_gain_one, grad_shift_one = first_pull(grad_normed_one)
+    tokens_grad = (grad_rows_in + grad_middle).astype(BF)
+
+    def scatter(g):
+        g = lax.psum_scatter(g.astype(BF), "dp", scatter_dimension=0, tiled=True)
+        return lax.psum_scatter(g, "fsdp", scatter_dimension=1, tiled=True).astype(F32)
+
+    small = (grad_project_bias, grad_output_bias, grad_expand_bias, grad_contract_bias,
+             grad_gain_one, grad_shift_one, grad_gain_two, grad_shift_two)
+    total = lax.psum(jnp.concatenate(small), ("dp", "fsdp"))
+    d = lax.axis_index("dp")
+    picked, at = [], 0
+    for item in small:
+        n = item.shape[0]
+        picked.append(lax.dynamic_slice(total, (at + d * (n // 8),), (n // 8,)))
+        at += n
+    return (block_out, tokens_grad, scatter(grad_project), picked[0], scatter(grad_output), picked[1],
+            scatter(grad_expand), picked[2], scatter(grad_contract), picked[3],
+            picked[4], picked[5], picked[6], picked[7])
+
+
 def solution(mesh):
-    placed = (
-        P(("dp", "fsdp"), None),
-        P(("dp", "fsdp")),
-        P(("dp", "fsdp"), None),
-        P("dp", "fsdp"),
-        P("dp"),
-        P("dp", "fsdp"),
-        P("dp"),
-        P("dp", "fsdp"),
-        P("dp"),
-        P("dp", "fsdp"),
-        P("dp"),
-        P("dp"),
-        P("dp"),
-        P("dp"),
-        P("dp"),
-    )
+    both, rows, grid = P(("dp", "fsdp"), None), P("dp"), P("dp", "fsdp")
+    weights = (grid, rows, grid, rows, grid, rows, grid, rows)
+    fast = mesh.shape["dp"] == 8 and mesh.shape["fsdp"] == 4
     return jax.shard_map(
-        per_device,
+        per_device_fast if fast else per_device,
         mesh=mesh,
-        in_specs=placed,
-        out_specs=(
-            P(("dp", "fsdp"), None),
-            P(("dp", "fsdp"), None),
-            P("dp", "fsdp"),
-            P("dp"),
-            P("dp", "fsdp"),
-            P("dp"),
-            P("dp", "fsdp"),
-            P("dp"),
-            P("dp", "fsdp"),
-            P("dp"),
-            P("dp"),
-            P("dp"),
-            P("dp"),
-            P("dp"),
-        ),
+        in_specs=(both, P(("dp", "fsdp")), both) + weights + (rows,) * 4,
+        out_specs=(both, both) + weights + (rows,) * 4,
         check_vma=False,
     )

time: 828 us -> 500 us (0.60)
  matrix products: 295 us -> 122 us
  Pallas kernels: 0 us -> 145 us
  waiting for transfers between devices: 195 us -> 92.2 us
  other arithmetic: 105 us -> 17.7 us
  blocking collectives: 133 us -> 60.7 us
  local copies, waits for them, and re-layouts: 73.2 us -> 40 us
    dot_general x14 -> x0, matrix products: 163 us -> none  [the longest x4 41.5 us: block_scores(): jnp.einsum('qhe,khe->hqk', query_block, keys_all, preferred_element_type=...]
    pallas_call x0 -> x2, Pallas kernels: none -> 145 us  [the longest x1 97.1 us: first_call(): pl.pallas_call(first_kernel, in_specs=[S, V, V, V, V, V], out_specs=[ANY]...]
    reduce_scatter x5, waiting for transfers between devices: 181 us -> 61.5 us  [the longest x4 40.5 us: scatter(): g = lax.psum_scatter(g.astype(BF), 'dp', scatter_dimension=0, tiled=True)]
    all_gather x5 -> x1, blocking collectives: 73.5 us -> 20.3 us  [per_device_fast(): wide = lax.all_gather(contract_weight, 'fsdp', axis=1, tiled=True)]
    convert_element_type x16 -> x3, other arithmetic: 55.6 us -> 3.01 us  [scatter(): lax.psum_scatter(g, 'fsdp', scatter_dimension=1, tiled=True).astype(F32)]
    unnamed x2 -> x0, blocking collectives: 47.2 us -> none
    psum x1, blocking collectives: 12.4 us -> 40.4 us  [per_device_fast(): total = lax.psum(jnp.concatenate(small), ('dp', 'fsdp'))]
    reduce_sum x5 -> x3, other arithmetic: 32.2 us -> 6.56 us  [the longest x1 3.04 us: per_device_fast(): column_sums = jnp.sum(grad_projected.astype(F32), axis=0)]
  transfers between devices with their start and end apart: 12 -> 9, of which waited for: 5 -> 5; matrix products, arithmetic and copies ran while one was open for 49% -> 35% of each run, Pallas kernels for 0% -> 29%
where the time goes in v1:
time: 500 us; the launch traced here: 494 us
  Pallas kernels  145 us (29%)
  matrix products  122 us (24%)
  waiting for transfers between devices  92.2 us (18%)
  blocking collectives  60.7 us (12%)
  local copies, waits for them, and re-layouts  40 us (8%)
  other arithmetic  17.7 us (4%)
  between operations  15.4 us (3%)
    pallas_call x1, Pallas kernels, first_call(): pl.pallas_call(first_kernel, in_specs=[S, V, V, V, V, V], out_specs=[ANY]...  97.1 us
    dot_general x3, matrix products, matmul(): return jnp.dot(first, second, preferred_element_type=jnp.float32)  49.4 us
    pallas_call x1, Pallas kernels, back_call(): pl.pallas_call(back_kernel, in_specs=[pl.BlockSpec(memory_space=pltpu.SME...  47.7 us
    dot_general x4, matrix products, over_columns(): lax.dot_general(first, second, (((1,), (1,)), ((), ())), preferred_elemen...  41.6 us
    reduce_scatter x4, waiting for transfers between devices, scatter(): g = lax.psum_scatter(g.astype(BF), 'dp', scatter_dimension=0, tiled=True)  40.5 us
    psum x1, blocking collectives, per_device_fast(): total = lax.psum(jnp.concatenate(small), ('dp', 'fsdp'))  40.4 us
    dot_general x4, matrix products, over_rows(): lax.dot_general(first, second, (((0,), (0,)), ((), ())), preferred_elemen...  31.2 us
    unnamed x12, waiting for transfers between devices  30.7 us
  transfers between devices with their start and end apart: 9, of which 5 were waited for; matrix products, arithmetic and copies ran while one was open for 35% of the time, Pallas kernels for 29%

profile of v1, /device:TPU:0, one launch (start us, length us, event | category | flops | bytes accessed | tf_op | source)
XLA Modules:
  0.0 493.6 jit_solution(9689307544902126456)
XLA Ops:
  7.2 20.3 %all_gather.6 = bf16[384,768]{0,1:T(8,128)(2,1)} all-gather(bf16[384,192]{0,1:T(8,128)(2,1)} %param.24), channel_id=1, replica_groups=mesh['dp'=8,'fsdp'=4] {'fsdp'}, dimensions={1}, use_global_device_ids=true | all-gather | bytes 737280 | tf_op jit(solution)/shard_map/all_gather | solution.py:809
  28.2 0.7 pad.27
  28.9 0.7 pad.28
  29.6 0.7 pad.29
  30.3 0.7 pad.30
  30.9 0.7 pad.31
  31.6 0.7 pad.32
  32.3 0.7 pad.33
  32.9 0.7 stack.29
  33.6 0.6 pad.34.vec_ref
  34.3 1.8 copy.39
  36.0 97.1 %first_part.1 = (bf16[1024,768]{1,0:T(8,128)(2,1)}, bf16[1024,2304]{1,0:T(8,128)(2,1)}, bf16[1024,768]{1,0:T(8,128)(2,1)}, bf16[12,1024,128]{2,1,0:T(8,128)(2,1)...) custom-call(s32[1]{0:T(128)} %copy.65.length_ref, ...), custom_call_target="tpu_custom_call" | custom-call | tf_op jit(solution)/shard_map/first_part/pallas_call | solution.py:374
  133.2 1.6 slice_reduce_fusion
  134.7 0.9 slice.27
  135.6 3.5 fusion.29
  139.6 1.3 copy-done.3
  140.9 36.4 %multiply_convert_fusion = (bf16[1024,3072]{1,0:T(8,128)(2,1)}, f32[1024,3072]{1,0:T(8,128)}, f32[1024,3072]{1,0:T(8,128)}) fusion(f32[3072]{0:T(1024)S(1)} %bitcast.33, bf16[768,3072]{1,0:T(8,128)(2,1)S(1)} %bitcast.36, f32[1024,768]{0,1:T(8,128)S(1)} %get-tuple-element.86, f32[768]{0:T(1024)S(1)} %get-tuple-element.66, f32[768]{0:T(1024)S(1)} %get-tuple-element.67, ...), kind=kOutput, calls=%fused_computation.4 | convolution fusion | flops 5043388416 | bytes 39348224 | tf_op jit(solution)/shard_map/dot_general | solution.py:413
  177.2 0.7 copy.41
  178.0 10.3 %convolution_convert_fusion = bf16[3072,768]{1,0:T(8,128)(2,1)} fusion(bf16[1024,3072]{1,0:T(8,128)(2,1)} %get-tuple-element.73, bf16[1024,768]{0,1:T(8,128)(2,1)S(1)} %copy.41, pred[1024]{0:T(1024)(128)(4,1)S(1)} %iota_compare_fusion), kind=kOutput, calls=%fused_computation.19 | convolution fusion | flops 4836556800 | bytes 12583936 | tf_op jit(solution)/shard_map/dot_general | solution.py:417
  188.4 16.9 %convert_reduce_fusion = (f32[3072]{0:T(1024)S(1)}, bf16[1024,3072]{1,0:T(8,128)(2,1)S(1)}) fusion(f32[1024,3072]{1,0:T(8,128)} %get-tuple-element.74, bf16[3072,768]{0,1:T(8,128)(2,1)} %all-gather.2.cloned.1.call-done, bf16[1024,768]{0,1:T(8,128)(2,1)S(1)} %copy.41, pred[1024]{0:T(1024)(128)(4,1)S(1)} %iota_compare_fusion, ...), kind=kOutput, calls=%fused_computation.2 | convolution fusion | flops 4887671808 | bytes 37774336 | tf_op jit(solution)/shard_map/dot_general | solution.py:423
  205.3 11.4 %fusion.31 = (f32[768]{0:T(1024)S(1)}, f32[1024,768]{1,0:T(8,128)}) fusion(bf16[1024,3072]{1,0:T(8,128)(2,1)S(1)} %get-tuple-element.89, bf16[768,3072]{1,0:T(8,128)(2,1)} %get-tuple-element.25), kind=kOutput, calls=%fused_computation.82 | convolution fusion | flops 4832623616 | bytes 14158848 | tf_op jit(solution)/shard_map/dot_general | solution.py:423
  216.7 3.9 copy.42
  220.7 3.0 multiply_reduce_fusion
  223.7 0.9 fusion.26
  224.6 0.5 copy-done.10
  225.1 0.6 convert_reduce_fusion.3
  225.7 0.5 copy-done.6
  226.2 1.1 copy-done.14
  227.3 2.5 convolution_convert_fusion.4
  229.9 4.4 convolution_convert_fusion.3.dm_ref
  234.2 47.7 %back_part.1 = bf16[1024,2304]{1,0:T(8,128)(2,1)} custom-call(s32[1]{0:T(128)} %copy.65.length_ref, bf16[1024,2304]{1,0:T(8,128)(2,1)} %get-tuple-element.26.proj_ref, bf16[1024,768]{1,0:T(8,128)(2,1)} %get-tuple-element.22.mixed_ref, bf16[12,1024,128]{2,1,0:T(8,128)(2,1)} %get-tuple-element.27.qa_ref, bf16[1024,768]{1,0:T(8,128)(2,1)} %convolution_convert_fusion.3.dm_ref), custom_call_target="tpu_custom_call" | custom-call | tf_op jit(solution)/shard_map/back_part/pallas_call | solution.py:796
  281.9 8.4 %convolution_convert_fusion.2 = bf16[768,2304]{1,0:T(8,128)(2,1)} fusion(bf16[1024,768]{1,0:T(8,128)(2,1)} %get-tuple-element.29, bf16[1024,2304]{1,0:T(8,128)(2,1)} %back_part.1), kind=kOutput, calls=%fused_computation.21 | convolution fusion | flops 3625648128 | bytes 9830400 | tf_op jit(solution)/shard_map/dot_general | solution.py:417
  290.7 2.1 copy.54
  292.9 10.0 %convolution_convert_fusion.1 = bf16[768,3072]{1,0:T(8,128)(2,1)} fusion(bf16[1024,3072]{1,0:T(8,128)(2,1)} %copy-done.17, f32[1024,768]{0,1:T(8,128)S(1)} %copy-done.4, f32[768]{0:T(1024)S(1)} %get-tuple-element.66, f32[768]{0:T(1024)S(1)} %get-tuple-element.67, f32[1024]{0:T(1024)S(1)} %fusion.20, f32[1024]{0:T(1024)S(1)} %broadcast_multiply_fusion.1), kind=kOutput, calls=%fused_computation.20 | convolution fusion | flops 4838129664 | bytes 14170112 | tf_op jit(solution)/shard_map/dot_general | solution.py:417
  303.0 1.3 copy-done.1
  304.7 9.0 %fusion.30 = (f32[768]{0:T(1024)S(1)}, f32[1024,768]{1,0:T(8,128)}) fusion(bf16[1024,2304]{1,0:T(8,128)(2,1)} %back_part.1, bf16[768,2304]{1,0:T(8,128)(2,1)} %get-tuple-element.28), kind=kOutput, calls=%fused_computation.81 | convolution fusion | flops 3624664320 | bytes 11406336 | tf_op jit(solution)/shard_map/dot_general | solution.py:423
  313.6 2.4 copy.43
  316.1 2.3 fusion.10
  318.4 1.3 fusion.13
  319.7 0.6 copy-done.7
  320.3 0.5 copy-done.11
  320.8 2.9 fusion.14
  323.7 1.7 copy.52
  325.5 3.0 convert_reduce_fusion.1
  328.5 9.0 %reduce-scatter.15.cloned.1.call-done = bf16[96,2304]{1,0:T(8,128)(2,1)} async-done(((bf16[768,2304]{1,0:T(8,128)(2,1)}), bf16[96,2304]{1,0:T(8,128)(2,1)}) %reduce-scatter.15.cloned.1.call-update) | async-done | bytes 442384 | tf_op jit(solution)/shard_map/reduce_scatter | solution.py:852
  337.6 2.1 copy.50
  339.8 40.4 %psum.7 = f32[9216]{0:T(1024)S(1)} all-reduce(f32[9216]{0:T(1024)S(1)} %constant_dynamic-update-slice_fusion), channel_id=1, replica_groups=mesh['dp'=8,'fsdp'=4] {'dp','fsdp'}, use_global_device_ids=true, to_apply=%region_18.19 | all-reduce | flops 9216 | bytes 73728 | tf_op jit(solution)/shard_map/psum | solution.py:857
  380.2 0.7 dynamic_slice.26
  380.8 0.6 dynamic_slice.24
  381.5 2.6 copy.47
  384.1 1.0 copy.55
  385.1 0.8 copy.48
  385.9 31.5 %reduce-scatter.19.cloned.1.call-done = bf16[96,3072]{1,0:T(8,128)(2,1)} async-done(((bf16[768,3072]{1,0:T(8,128)(2,1)}), bf16[96,3072]{1,0:T(8,128)(2,1)}) %reduce-scatter.19.cloned.1.call-update) | async-done | bytes 589840 | tf_op jit(solution)/shard_map/reduce_scatter | solution.py:852
  417.5 9.5 %select_convert_fusion = bf16[1024,768]{0,1:T(8,128)(2,1)} fusion(f32[1024,768]{0,1:T(8,128)S(1)} %copy-done.5, bf16[1024,3072]{1,0:T(8,128)(2,1)} %get-tuple-element.73, bf16[3072,768]{0,1:T(8,128)(2,1)} %all-gather.2.cloned.1.call-done, f32[768]{0:T(1024)S(1)} %copy-done.16, pred[1024]{0:T(1024)(128)(4,1)S(1)} %iota_compare_fusion), kind=kOutput, calls=%fused_computation.43 | convolution fusion | flops 4834983936 | bytes 15732736 | tf_op jit(solution)/shard_map/dot_general | solution.py:413
  427.0 2.6 copy.46
  429.6 0.6 fusion.28
  430.2 9.6 %reduce-scatter.27.cloned.1.call-done = bf16[192,96]{1,0:T(8,128)(2,1)} async-done(((bf16[768,96]{1,0:T(8,128)(2,1)}), bf16[192,96]{1,0:T(8,128)(2,1)}) %reduce-scatter.27.cloned.1.call-update) | async-done | bytes 36880
  439.7 0.9 copy.53
  440.6 0.6 convert_element_type.90
  441.3 21.0 %reduce-scatter.25.cloned.1.call-done = bf16[576,96]{1,0:T(8,128)(2,1)} async-done(((bf16[2304,96]{1,0:T(8,128)(2,1)}), bf16[576,96]{1,0:T(8,128)(2,1)}) %reduce-scatter.25.cloned.1.call-update) | async-done | bytes 110608
  462.2 1.0 copy.51
  463.3 0.7 convert_element_type.85
  464.0 20.9 %reduce-scatter.21.cloned.1.call-done = bf16[96,768]{1,0:T(8,128)(2,1)} async-done(((bf16[96,3072]{1,0:T(8,128)(2,1)}), bf16[96,768]{1,0:T(8,128)(2,1)}) %reduce-scatter.21.cloned.1.call-update) | async-done | bytes 147472 | tf_op jit(solution)/shard_map/reduce_scatter | solution.py:853
  485.0 1.6 convert_element_type.92
  (84 shorter events, 1.7 us)
Async XLA Ops:
  7.2 181.2 %all-gather.2.cloned.1.call-start = ((), (), s32[]{:S(2)}) async-start(), calls=%async_computation.8 | async-start | bytes 5308416 | tf_op jit(solution)/shard_map/all_gather | solution.py:810
  27.5 263.2 %reduce-scatter.23.cloned.1.call-start = ((), (), s32[]{:S(2)}) async-start(), calls=%async_computation.13 | async-start | bytes 5308416 | tf_op jit(solution)/shard_map/reduce_scatter | solution.py:852
  36.0 103.2 %copy-start = (bf16[1024,768]{0,1:T(8,128)(2,1)}, bf16[1024,768]{0,1:T(8,128)(2,1)S(1)}, u32[]{:S(2)}) copy-start(bf16[1024,768]{0,1:T(8,128)(2,1)S(1)} %copy.39) | copy-start | bytes 4718596
  135.6 5.2 %slice-start = ((s8[4718592]{0:T(1024)(128)(4,1)}), s8[4194304]{0:T(1024)(128)(4,1)S(1)}, s32[]{:S(2)}) async-start(s8[4718592]{0:T(1024)(128)(4,1)} %bitcast.35), calls=%async_computation.17 | async-start | bytes 8388608
  135.6 5.2 %slice-start.1 = ((s8[4718592]{0:T(1024)(128)(4,1)}), s8[524288]{0:T(1024)(128)(4,1)S(1)}, s32[]{:S(2)}) async-start(s8[4718592]{0:T(1024)(128)(4,1)} %bitcast.35), calls=%async_computation.18 | async-start | bytes 1048576
  139.2 1.7 copy-start.3
  140.9 36.4 %copy-start.13 = (bf16[1024,768]{1,0:T(8,128)(2,1)S(1)}, bf16[1024,768]{1,0:T(8,128)(2,1)}, u32[]{:S(2)}) copy-start(bf16[1024,768]{1,0:T(8,128)(2,1)} %param.17) | copy-start | bytes 4718596
  178.0 10.4 %copy-start.9 = (bf16[1024,768]{0,1:T(8,128)(2,1)}, bf16[1024,768]{0,1:T(8,128)(2,1)S(1)}, u32[]{:S(2)}) copy-start(bf16[1024,768]{0,1:T(8,128)(2,1)S(1)} %copy.41) | copy-start | bytes 4718596
  188.3 135.3 %reduce-scatter.17.cloned.1.call-start = ((), (), s32[]{:S(2)}) async-start(), calls=%async_computation.10 | async-start | bytes 1327104 | tf_op jit(solution)/shard_map/reduce_scatter | solution.py:852
  205.3 11.4 %copy-start.17 = (bf16[1024,3072]{1,0:T(8,128)(2,1)}, bf16[1024,3072]{1,0:T(8,128)(2,1)S(1)}, u32[]{:S(2)}) copy-start(bf16[1024,3072]{1,0:T(8,128)(2,1)S(1)} %get-tuple-element.89) | copy-start | bytes 18874372
  216.7 3.9 copy-start.4
  220.6 3.0 copy-start.8
  223.6 1.4 copy-start.10
  224.5 1.7 copy-start.6
  225.1 2.3 copy-start.12
  226.2 1.1 copy-start.14
  229.8 107.7 %reduce-scatter.15.cloned.1.call-start = ((), (), s32[]{:S(2)}) async-start(), calls=%async_computation.9 | async-start | bytes 3981312 | tf_op jit(solution)/shard_map/reduce_scatter | solution.py:852
  290.4 93.7 %reduce-scatter.29.cloned.1.call-start = ((), (), s32[]{:S(2)}) async-start(), calls=%async_computation.16 | async-start | bytes 737280
  292.9 124.5 %reduce-scatter.19.cloned.1.call-start = ((), (), s32[]{:S(2)}) async-start(), calls=%async_computation.11 | async-start | bytes 5308416 | tf_op jit(solution)/shard_map/reduce_scatter | solution.py:852
  302.9 1.4 copy-start.1
  303.0 136.8 %reduce-scatter.27.cloned.1.call-start = ((), (), s32[]{:S(2)}) async-start(), calls=%async_computation.15 | async-start | bytes 245760
  313.6 2.4 copy-start.15
  316.0 2.3 copy-start.2
  318.3 1.9 copy-start.7
  318.3 2.4 copy-start.11
  325.4 136.8 %reduce-scatter.25.cloned.1.call-start = ((), (), s32[]{:S(2)}) async-start(), calls=%async_computation.14 | async-start | bytes 737280
  328.5 88.9 %copy-start.5 = (f32[1024,768]{0,1:T(8,128)S(1)}, f32[1024,768]{0,1:T(8,128)}, u32[]{:S(2)}) copy-start(f32[1024,768]{0,1:T(8,128)} %copy-done.3) | copy-start | bytes 9437188
  328.5 88.9 %copy-start.16 = (f32[768]{0:T(1024)S(1)}, f32[768]{0:T(1024)}, u32[]{:S(2)}) copy-start(f32[768]{0:T(1024)} %get-tuple-element.65) | copy-start | bytes 9220
  339.7 145.3 %reduce-scatter.21.cloned.1.call-start = ((), (), s32[]{:S(2)}) async-start(), calls=%async_computation.12 | async-start | bytes 737280 | tf_op jit(solution)/shard_map/reduce_scatter | solution.py:853
Sparse Core Ops, SparseCore 0:
  27.7 48.5 all-gather.1
  188.5 53.1 reduce-scatter.22
  245.2 36.7 reduce-scatter.16
  290.5 46.9 reduce-scatter.14
  339.7 22.0 reduce-scatter.28
  365.1 52.2 reduce-scatter.18
  420.3 19.3 reduce-scatter.26
  442.0 20.1 reduce-scatter.24
  464.5 20.3 reduce-scatter.20

commit v2 on v1

--- a/solution.py
+++ b/solution.py
@@ -57,6 +57,8 @@
             return (self.dy, self.z)
         if to == "c":
             return (self.dc, self.z)
+        if isinstance(to, tuple):
+            return (self.d, to[1])
         return (self.d, self.zt(to))
 
 
@@ -745,125 +747,556 @@
     )
 
 
-def back_kernel(length_ref, proj_ref, mixed_ref, qa_ref, dm_ref, dproj_ref, ka_ref, da_ref, dq_ref, va_ref, kT_ref):
+def scatter_events(link, place, col, pair_of, block_of, lc, lxh, lyh, lx, ly, lz, finish):
+    p = place
+    family = (p.dc, p.dx + p.dc - p.d, p.dy + p.dc - p.d, p.dd + p.dc - p.d)
+    cs = [link.slot() for _ in range(4)]
+    hx, hy, fx, fy = (link.slot() for _ in range(4))
+    zs = [link.slot() for _ in range(4)]
+    got = link.got
+
+    def add(target, *terms):
+        total = target[...].astype(F32)
+        for term in terms:
+            total = total + term[...].astype(F32)
+        target[...] = total.astype(BF)
+
+    def to_sibling(which):
+        link.send(cs[which], col(family[which]), lc.at[which], "c", lambda: col(0))
+
+    def halves():
+        got(cs[3], lc.at[3])
+        add(col(p.dd), lc.at[3])
+        link.send(hx, pair_of(col(p.dd), 0), lxh, "x", lambda: lxh)
+        link.send(hy, pair_of(col(p.dd), 1), lyh, "y", lambda: lyh)
+
+    def near():
+        got(cs[1], lc.at[1])
+        got(cs[2], lc.at[2])
+        add(col(p.dx), lc.at[1])
+        add(col(p.dy), lc.at[2])
+
+    def pass_y():
+        got(hx, lxh)
+        add(pair_of(col(p.dy), 0), lxh)
+        link.send(fy, col(p.dy), ly, "y", lambda: ly)
+
+    def pass_x():
+        got(hy, lyh)
+        add(pair_of(col(p.dx), 1), lyh)
+        link.send(fx, col(p.dx), lx, "x", lambda: lx)
+
+    def own():
+        got(cs[0], lc.at[0])
+
+    def along_z():
+        got(fx, lx)
+        got(fy, ly)
+        add(col(p.d), lc.at[0], lx, ly)
+        for step in (1, 3, 2) if lz is not None else ():
+            link.send(zs[step], block_of(col(p.d), p.zt(step)), lz.at[step], step, lambda: lz.at[0])
+
+    def last():
+        total = block_of(col(p.d), p.z)[...].astype(F32)
+        for step in (1, 3, 2):
+            got(zs[step], lz.at[step])
+            total = total + lz[step].astype(F32)
+        finish(total)
+
+    return to_sibling, [halves, near, pass_y, pass_x, own, along_z, last]
+
+
+def gelu_pair(value):
+    lift = 0.5 * (1.0 + lax.erf(value * 0.7071067811865476))
+    bell = jnp.exp(value * value * -0.5) * 0.3989422804014327
+    return value * lift, lift + value * bell
+
+
+def second_kernel(length_ref, x_ref, cot_ref, mixed_ref, wo_ref, we_hbm, wc_ref, v_ref,
+                  block_out, dmixed_out, dmiddle_out, ge_out, go_out, gc_out, vg_out,
+                  we, wct, act, slope, middle, n2t, dot_t, mixed_t, dbranch, dout, gc, go, dmixed, bout, vg,
+                  lc, lxh, lyh, lx, ly, lz, send_sem, recv_sem, out_sem):
+    p = Place()
+    T, D = x_ref.shape
+    FF = we.shape[1]
+    R = D // 8
+    Q = FF // 4
+    C8 = FF // 8
+    link = Link(p, send_sem, recv_sem)
+    bc = lambda z, d: wct.at[pl.ds(mo(z * (D // 4), 16), D // 4), pl.ds(mo(d * C8, 128), C8)]
+    gather = gather_events(link, p, bc)
+
+    def finish(total):
+        gc_out[...] = total.T
+
+    to_sibling, scatter = scatter_events(
+        link, p, lambda d: gc.at[d], lambda ref, h: ref.at[pl.ds(2 * h, 2)], lambda ref, z: ref.at[z],
+        lc, lxh, lyh, lx, ly, lz, finish)
+    load = pltpu.make_async_copy(we_hbm, we, out_sem.at[0])
+    load.start()
+    wct[pl.ds(mo(p.z * (D // 4), 16), D // 4), pl.ds(mo(p.d * C8, 128), C8)] = wc_ref[...].astype(F32).T.astype(BF)
+    enter(p)
+    gather[0]()
     length = length_ref[0]
-    T, D = mixed_ref.shape
+    LR = 256
+    rows = lambda i: pl.ds(mo(i * LR, LR), LR)
+    vec = lambda i: v_ref[i:i + 1, 0:D]
+    vg[...] = jnp.zeros_like(vg)
+
+    def at(i, spots):
+        for where, event in spots:
+            pl.when(i == where)(event)
+
+    def norm(value):
+        u = value - jnp.mean(value, axis=-1, keepdims=True)
+        r = lax.rsqrt(jnp.mean(u * u, axis=-1, keepdims=True) + eps_norm)
+        return u * r, r
+
+    def middle_body(i, _):
+        at(i, [(1, gather[1]), (3, gather[2])])
+        r = rows(i)
+        value = x_ref[r, :].astype(F32) + (dot(mixed_ref[r, :], wo_ref[...]) + vec(2))
+        middle[r, :] = value
+        xhat, _ = norm(value)
+        n2 = (xhat * vec(6) + vec(7)).astype(BF)
+        dmixed[r, :] = n2
+        n2t[:, r] = n2.T
+        live = iota((LR, D), 0) + i * LR < length
+        grad = jnp.where(live, cot_ref[r, :].astype(F32), 0.0)
+        vg[7:8, :] += jnp.sum(grad, axis=0, keepdims=True)
+        dout[r, :] = grad.astype(BF)
+        dot_t[:, r] = grad.astype(BF).T
+        mixed_t[:, r] = mixed_ref[r, :].T
+        return 0
+
+    lax.fori_loop(0, T // LR, middle_body, 0)
+    load.wait()
+
+    def hidden_body(i, _):
+        at(i, [(0, gather[3]), (1, gather[4]), (1, gather[5]), (2, gather[6]), (2, gather[7]), (3, gather[8]),
+               (3, gather[9])])
+        r = rows(i)
+        left = dmixed[r, :]
+        for j in range(4):
+            cols = slice(j * Q, (j + 1) * Q)
+            first, second = gelu_pair(dot(left, we[:, cols]) + v_ref[1:2, cols])
+            act[r, cols] = first.astype(BF)
+            slope[r, cols] = second.astype(BF)
+        return 0
+
+    lax.fori_loop(0, T // LR, hidden_body, 0)
+    gather[10]()
+
+    def column(d):
+        value = dot(dot_t[...], act[:, pl.ds(mo(d * C8, 128), C8)])
+        gc[d] = value.reshape(4, D // 4, C8).astype(BF)
+
+    sib = p.dc - p.d
+    column(p.dd + sib)
+    to_sibling(3)
+    column(p.dd)
+    gather[11]()
+    column(p.dx + sib)
+    to_sibling(1)
+    column(p.dy + sib)
+    to_sibling(2)
+    scatter[0]()
+    column(p.dx)
+    column(p.dy)
+    scatter[1]()
+    column(p.d + sib)
+    to_sibling(0)
+    column(p.d)
+    gather[12]()
+
+    def back_body(i, _):
+        at(i, [(0, scatter[2]), (0, scatter[3]), (1, scatter[4]), (3, scatter[5])])
+        r = rows(i)
+        grad_low = dout[r, :]
+        result = middle[r, :] + vec(3)
+        dn = jnp.zeros((LR, D), F32)
+        for j in range(4):
+            cols = slice(j * Q, (j + 1) * Q)
+            dh = dot(grad_low, wct[:, cols]) * slope[r, cols].astype(F32)
+            low = dh.astype(BF)
+            slope[r, cols] = low
+            vg[3 + j:4 + j, :] += jnp.sum(low.astype(F32), axis=0, keepdims=True)
+            result = result + dot_nt(act[r, cols], wct[:, cols])
+            dn = dn + dot_nt(low, we[:, cols])
+        live = iota((LR, D), 0) + i * LR < length
+        bout[r, :] = jnp.where(live, result, 0.0).astype(BF)
+        xhat, spread = norm(middle[r, :])
+        vg[10:11, :] += jnp.sum(dn * xhat, axis=0, keepdims=True)
+        vg[11:12, :] += jnp.sum(dn, axis=0, keepdims=True)
+        gx = dn * vec(6)
+        back = spread * (gx - jnp.mean(gx, axis=-1, keepdims=True)
+                         - xhat * jnp.mean(gx * xhat, axis=-1, keepdims=True))
+        total = dout[r, :].astype(F32) + back
+        middle[r, :] = total
+        branch = total.astype(BF)
+        dbranch[r, :] = branch
+        vg[2:3, :] += jnp.sum(branch.astype(F32), axis=0, keepdims=True)
+        dmixed[r, :] = dot_nt(branch, wo_ref[...]).astype(BF)
+        return 0
+
+    lax.fori_loop(0, T // LR, back_body, 0)
+    outs = []
+
+    def out(source, target):
+        made = pltpu.make_async_copy(source, target, out_sem.at[1 + len(outs)])
+        made.start()
+        outs.append(made)
+
+    out(bout, block_out)
+    out(dmixed, dmixed_out)
+    out(middle, dmiddle_out)
+    for z in range(4):
+        act[0:D, z * Q:(z + 1) * Q] = dot(n2t[...], slope[:, z * Q:(z + 1) * Q]).astype(BF)
+    out(act.at[0:D, :], ge_out)
+    for z in range(4):
+        cols = slice(3 * z // 2 * 128, 3 * z // 2 * 128 + 256)
+        go[:, z] = dot(mixed_t[...], dbranch[:, cols]).reshape(8, R, 256).astype(BF)
+    out(go, go_out)
+    vg_out[...] = vg[...]
+    scatter[6]()
+    link.finish()
+    for made in outs:
+        made.wait()
+
+
+ANY = pl.BlockSpec(memory_space=pl.ANY)
+VM = pl.BlockSpec(memory_space=pltpu.VMEM)
+SM = pl.BlockSpec(memory_space=pltpu.SMEM)
+sds = jax.ShapeDtypeStruct
+
+
+def second_call(length, x, cot, mixed, wo, we, wc, v):
+    T, D = x.shape
+    FF = we.shape[1]
+    n = 32 + 12
+    R, C8, Z = D // 8, FF // 8, D // 4
+    vm = pltpu.VMEM
+    return pl.pallas_call(
+        second_kernel,
+        in_specs=[SM, VM, VM, VM, VM, ANY, VM, VM],
+        out_specs=[ANY] * 5 + [VM] * 2,
+        out_shape=[sds((T, D), BF), sds((T, D), BF), sds((T, D), F32), sds((D, FF), BF), sds((8, 4, R, 256), BF),
+                   sds((C8, Z), F32), sds((16, D), F32)],
+        scratch_shapes=[
+            vm((D, FF), BF), vm((D, FF), BF), vm((T, FF), BF), vm((T, FF), BF), vm((T, D), F32),
+            vm((D, T), BF), vm((D, T), BF), vm((D, T), BF), vm((T, D), BF), vm((T, D), BF),
+            vm((8, 4, Z, C8), BF), vm((8, 4, R, 256), BF), vm((T, D), BF), vm((T, D), BF), vm((16, D), F32),
+            vm((4, 4, Z, C8), BF), vm((2, Z, C8), BF), vm((2, Z, C8), BF), vm((4, Z, C8), BF), vm((4, Z, C8), BF),
+            vm((4, Z, C8), BF),
+            pltpu.SemaphoreType.DMA((n,)), pltpu.SemaphoreType.DMA((n,)), pltpu.SemaphoreType.DMA((6,)),
+        ],
+        compiler_params=pltpu.CompilerParams(
+            collective_id=1, has_side_effects=True, vmem_limit_bytes=62 << 20),
+        name="second_part",
+    )(length, x, cot, mixed, wo, we, wc, v)
+
+
+def third_kernel(length_ref, proj_hbm, qa_hbm, mixed_hbm, dm_hbm, n1_hbm, wp_hbm, x_hbm, dmiddle_hbm, ge_hbm, go_hbm,
+                 vg_ref, v_ref,
+                 tokens_out, gp_out, go_out, ge_out, vec_out,
+                 proj, qa, mixed, dm, n1, n1t, wpp, x, dmiddle, ge, go, dproj, tg, gp,
+                 ka, da, dq, va, kt, vs, vl,
+                 lce, lxhe, lyhe, lxe, lye, lze, lco, lxho, lyho, lxo, lyo, lzo,
+                 lcp, lxhp, lyhp, lxp, lyp, lzp, gpw,
+                 send_sem, recv_sem, load_sem):
+    p = Place()
+    T, D = x.shape
+    FF = ge.shape[1]
+    R = D // 8
+    Q = FF // 4
+    pairs = H // 2
     KB = 256
-
-    def pair_body(p, _):
-        lane, row = iota((T, 128), 1), iota((T, 128), 0)
-        ps = lambda off: pl.ds(mo(off + p * 128, 128), 128)
-        k = proj_ref[:, ps(D)].astype(F32)
-        v = proj_ref[:, ps(2 * D)].astype(F32)
-        do = dm_ref[:, ps(0)].astype(F32)
-        pr = do * mixed_ref[:, ps(0)].astype(F32)
-        dead = jnp.where(row < length, 0.0, neg_fill)
+    parts = T // KB
+    link = Link(p, send_sem, recv_sem)
+    loads = []
+
+    def load(source, target):
+        made = pltpu.make_async_copy(source, target, load_sem.at[len(loads)])
+        made.start()
+        loads.append(made)
+        return made
+
+    first_loads = [load(a, b) for a, b in ((proj_hbm, proj), (qa_hbm, qa), (mixed_hbm, mixed), (dm_hbm, dm))]
+    ge_load, go_load, n1_load = load(ge_hbm, ge), load(go_hbm, go), load(n1_hbm, n1)
+    late = [load(x_hbm, x), load(dmiddle_hbm, dmiddle)]
+    for i in range(pairs):
+        for s in range(3):
+            late.append(load(wp_hbm.at[:, pl.ds((s * pairs + i) * 128, 128)],
+                             wpp.at[:, pl.ds((i * 3 + s) * 128, 128)]))
+
+    def finish_e(total):
+        ge_out[...] = total
+
+    def finish_o(total):
+        go_out[...] = jnp.where(p.odd == 0, total[:, 0:192], total[:, 64:256])
+
+    rows_of = lambda d: pl.ds(mo(d * R, 16), R)
+    e_sib, ev_e = scatter_events(
+        link, p, lambda d: ge.at[rows_of(d), :], lambda ref, h: ref.at[:, pl.ds(h * (FF // 2), FF // 2)],
+        lambda ref, z: ref.at[:, pl.ds(mo(z * Q, 128), Q)], lce, lxhe, lyhe, lxe, lye, lze, finish_e)
+    o_sib, ev_o = scatter_events(
+        link, p, lambda d: go.at[d], lambda ref, h: ref.at[pl.ds(2 * h, 2)], lambda ref, z: ref.at[z],
+        lco, lxho, lyho, lxo, lyo, lzo, finish_o)
+    ended = []
+    combos = []
+    for i in range(pairs):
+        for s in range(3):
+            tile = s * pairs + i
+            for owner in range(4):
+                left = 9 * owner // 2
+                if left <= tile < left + 5:
+                    combos.append((i, s, owner, tile - left))
+    assert len(combos) == 20
+    z_slots = [[link.slot() for _ in range(3)] for _ in combos]
+
+    def pair_scatter(i):
+        column = lambda d: gp.at[i, d]
+        sib, events = scatter_events(
+            link, p, column, lambda ref, h: ref.at[pl.ds(h * (R // 2), R // 2)], None,
+            lcp.at[i], lxhp.at[i], lyhp.at[i], lxp.at[i], lyp.at[i], None, None)
+        mine = [(at, c) for at, c in enumerate(combos) if c[0] == i]
+
+        def along(add_own):
+            def run():
+                add_own()
+                for at, (_, s, owner, _) in mine:
+                    @pl.when(p.z != owner)
+                    def _():
+                        step = lax.rem(owner - p.z + 4, 4)
+                        part = column(p.d).at[:, pl.ds(s * 128, 128)]
+                        link.copy(z_slots[at][0] + step - 1, part, lzp.at[at, step - 1], ("z", owner)).start()
+            return run
+
+        def last():
+            for at, (_, s, owner, place) in mine:
+                @pl.when(p.z == owner)
+                def _():
+                    total = gp[i, p.d, :, s * 128:(s + 1) * 128].astype(F32)
+                    for step in range(1, 4):
+                        link.got(z_slots[at][step - 1], lzp.at[at, step - 1])
+                        total = total + lzp[at, step - 1].astype(F32)
+                    gpw[:, place * 128:(place + 1) * 128] = total
+
+        def ending():
+            for at, (_, s, owner, _) in mine:
+                @pl.when(p.z != owner)
+                def _():
+                    step = lax.rem(owner - p.z + 4, 4)
+                    view = lzp.at[at, 0]
+                    link.copy(z_slots[at][0] + step - 1, view, view, "x").wait_send()
+
+        ended.append(ending)
+
+        def start():
+            for k in (3, 1, 2, 0):
+                sib(k)
+
+        return [start] + events[:5] + [along(events[5]), last]
+
+    ev_p = [pair_scatter(i) for i in range(pairs)]
+
+    enter(p)
+    for made in first_loads:
+        made.wait()
+    length = length_ref[0]
+
+    def start_e():
+        ge_load.wait()
+        for k in (3, 1, 2, 0):
+            e_sib(k)
+
+    def start_o():
+        go_load.wait()
+        for k in (3, 1, 2, 0):
+            o_sib(k)
+
+    def turn_n1():
+        n1_load.wait()
+        for i in range(T // 256):
+            n1t[:, i * 256:(i + 1) * 256] = n1[i * 256:(i + 1) * 256, :].T
+
+    timeline = [(0, start_e), (1, turn_n1), (3, ev_e[0]), (3, ev_e[1]), (7, ev_e[2]), (7, ev_e[3]), (8, ev_e[4]),
+                (9, start_o), (10, ev_o[0]), (10, ev_o[1]),
+                (14, ev_e[5]), (15, ev_o[2]), (15, ev_o[3]), (15, ev_o[4]), (17, ev_o[5]), (20, ev_o[6]), (21, ev_e[6])]
+    for i in range(pairs - 1):
+        base = max(4 * (i + 1), 9)
+        for k, event in enumerate(ev_p[i]):
+            spot = {0: base, 1: base + 2, 2: base + 2, 3: base + 4, 4: base + 4, 5: base + 4, 6: base + 6, 7: base + 9}[k]
+            timeline.append((spot, event))
+    timeline.sort(key=lambda e: e[0])
+
+    def body(step, _):
+        for at, event in timeline:
+            if at < pairs * parts:
+                pl.when(step == at)(event)
+        pair = lax.div(step, parts)
+        part = lax.rem(step, parts)
+        ps = lambda off: pl.ds(mo(off + pair * 128, 128), 128)
+        own = lambda s: pl.ds(mo(pair * 384 + s * 128, 128), 128)
+
+        @pl.when(part == 0)
+        def _():
+            lane, row = iota((T, 128), 1), iota((T, 128), 0)
+            k = proj[:, ps(D)].astype(F32)
+            v = proj[:, ps(2 * D)].astype(F32)
+            do = dm[:, ps(0)].astype(F32)
+            pr = do * mixed[:, ps(0)].astype(F32)
+            dead = jnp.where(row < length, 0.0, neg_fill)
+            for head in range(2):
+                keep = (lane < 64) if head == 0 else (lane >= 64)
+                delta = jnp.sum(jnp.where(keep, pr, 0.0), axis=-1, keepdims=True)
+                one, two, three = split3(-delta)
+                da[head] = extend(head, do, lane, one, two, three, 0.0)
+                ka[head] = extend(head, k, lane, 1.0, 1.0, 1.0, dead)
+                va[head] = extend(head, v, lane, 1.0, 1.0, 1.0, 0.0)
+                kt[head] = jnp.where(keep, k, 0.0).astype(BF).T
+            dq[...] = jnp.zeros_like(dq)
+
+        r = pl.ds(mo(part * KB, KB), KB)
+        lk = iota((KB, 128), 1)
+        dks, dvs = [], []
         for head in range(2):
-            keep = (lane < 64) if head == 0 else (lane >= 64)
-            delta = jnp.sum(jnp.where(keep, pr, 0.0), axis=-1, keepdims=True)
-            one, two, three = split3(-delta)
-            da_ref[head] = extend(head, do, lane, one, two, three, 0.0)
-            ka_ref[head] = extend(head, k, lane, 1.0, 1.0, 1.0, dead)
-            va_ref[head] = extend(head, v, lane, 1.0, 1.0, 1.0, 0.0)
-            kT_ref[head] = jnp.where(keep, k, 0.0).astype(BF).T
-        dq_ref[...] = jnp.zeros_like(dq_ref)
-
-        def kblk(i, _):
-            rows = pl.ds(mo(i * KB, KB), KB)
-            lk = iota((KB, 128), 1)
-            dks, dvs = [], []
-            for head in range(2):
-                weights = jnp.exp(dot_nt(ka_ref[head, rows, :], qa_ref[p * 2 + head]))
-                low = weights.astype(BF)
-                ds = (weights * dot_nt(va_ref[head, rows, :], da_ref[head])).astype(BF)
-                dvs.append(dot(low, da_ref[head]))
-                dks.append(dot(ds, qa_ref[p * 2 + head]))
-                dq_ref[head] += dot(kT_ref[head, :, rows], ds)
-            dproj_ref[rows, ps(D)] = jnp.where(lk < 64, dks[0], dks[1]).astype(BF)
-            dproj_ref[rows, ps(2 * D)] = jnp.where(lk < 64, dvs[0], dvs[1]).astype(BF)
-            return 0
-
-        lax.fori_loop(0, T // KB, kblk, 0)
-        dproj_ref[:, ps(0)] = ((dq_ref[0] + dq_ref[1]) * (HD ** -0.5)).T.astype(BF)
+            weights = jnp.exp(dot_nt(ka[head, r, :], qa[pair * 2 + head]))
+            low = weights.astype(BF)
+            ds = (weights * dot_nt(va[head, r, :], da[head])).astype(BF)
+            dvs.append(dot(low, da[head]))
+            dks.append(dot(ds, qa[pair * 2 + head]))
+            dq[head] += dot(kt[head, :, r], ds)
+        dproj[r, own(1)] = jnp.where(lk < 64, dks[0], dks[1]).astype(BF)
+        dproj[r, own(2)] = jnp.where(lk < 64, dvs[0], dvs[1]).astype(BF)
+
+        @pl.when(part == parts - 1)
+        def _():
+            dproj[:, own(0)] = ((dq[0] + dq[1]) * (HD ** -0.5)).T.astype(BF)
+            value = dot(n1t[...], dproj[:, pl.ds(mo(pair * 384, 128), 384)])
+            gp[pair] = value.reshape(8, R, 384).astype(BF)
+
         return 0
 
-    lax.fori_loop(0, H // 2, pair_body, 0)
-
-
-def back_call(length, proj, mixed, qa, dm):
-    T, D = mixed.shape
-    V = pl.BlockSpec(memory_space=pltpu.VMEM)
+    lax.fori_loop(0, pairs * parts, body, 0)
+    tail = [e for at, e in timeline if at >= pairs * parts]
+    ev_p[pairs - 1][0]()
+    for made in late:
+        made.wait()
+    vs[...] = vg_ref[...]
+    LR = 256
+
+    def norm_body(i, _):
+        def spot(where, events):
+            @pl.when(i == where)
+            def _():
+                for event in events:
+                    event()
+
+        spot(1, ev_p[pairs - 1][1:3])
+        spot(2, ev_p[pairs - 1][3:6])
+        r = pl.ds(mo(i * LR, LR), LR)
+        left = dproj[r, :]
+        dn = dot_nt(left, wpp[...])
+        sums = jnp.sum(left.astype(F32), axis=0, keepdims=True)
+        for j in range(pairs):
+            vs[0:1, j * 128:(j + 1) * 128] += sums[:, j * 384:j * 384 + 128]
+            vs[1:2, j * 128:(j + 1) * 128] += sums[:, j * 384 + 256:j * 384 + 384]
+        value = x[r, :].astype(F32)
+        u = value - jnp.mean(value, axis=-1, keepdims=True)
+        spread = lax.rsqrt(jnp.mean(u * u, axis=-1, keepdims=True) + eps_norm)
+        xhat = u * spread
+        vs[8:9, :] += jnp.sum(dn * xhat, axis=0, keepdims=True)
+        vs[9:10, :] += jnp.sum(dn, axis=0, keepdims=True)
+        gx = dn * v_ref[4:5, 0:D]
+        back = spread * (gx - jnp.mean(gx, axis=-1, keepdims=True)
+                         - xhat * jnp.mean(gx * xhat, axis=-1, keepdims=True))
+        tg[r, :] = (back + dmiddle[r, :]).astype(BF)
+        return 0
+
+    lax.fori_loop(0, T // LR, norm_body, 0)
+    out = load(tg, tokens_out)
+    v_slots = [link.slot() for _ in range(6)]
+    link.send(v_slots[0], vs, vl.at[0], "c", lambda: vl.at[0])
+    for event in tail:
+        event()
+    ev_p[pairs - 1][6]()
+    link.got(v_slots[0], vl.at[0])
+    vl[6] = vs[...] + vl[0]
+    link.send(v_slots[1], vl.at[6], vl.at[1], "x", lambda: vl.at[0])
+    link.got(v_slots[1], vl.at[1])
+    vl[7] = vl[6] + vl[1]
+    link.send(v_slots[2], vl.at[7], vl.at[2], "y", lambda: vl.at[0])
+    link.got(v_slots[2], vl.at[2])
+    vl[8] = vl[7] + vl[2]
+    for step in (1, 3, 2):
+        link.send(v_slots[2 + step], vl.at[8], vl.at[2 + step], step, lambda: vl.at[0])
+    ev_p[pairs - 1][7]()
+    gp_out[...] = jnp.where(p.odd == 0, gpw[:, 0:576], gpw[:, 64:640])
+    for step in (1, 3, 2):
+        link.got(v_slots[2 + step], vl.at[2 + step])
+    total = vl[8] + vl[3] + vl[4] + vl[5]
+    quarter, half = lax.div(p.d, 4), lax.div(p.d, 2)
+    pb = jnp.where(quarter == 0, total[0:1], total[1:2])
+    eb = jnp.where(half < 2, jnp.where(half == 0, total[3:4], total[4:5]), jnp.where(half == 2, total[5:6], total[6:7]))
+    plain = jnp.concatenate([total[2:3], total[7:12], total[2:4]], axis=0)
+    turn = lambda value, by: pltpu.roll(value, lax.rem(D - by, D), 1)
+    wide8 = lambda value: jnp.broadcast_to(value, (8, D))
+    vec_out[0] = turn(plain, p.d * R)[:, 0:384]
+    vec_out[1] = turn(wide8(pb), lax.rem(p.d, 4) * 2 * R)[:, 0:384]
+    vec_out[2] = turn(wide8(eb), lax.rem(p.d, 2) * 4 * R)[:, 0:384]
+    link.finish()
+    for ending in ended:
+        ending()
+    out.wait()
+
+
+def third_call(length, proj, qa, mixed, dm, n1, wp, x, dmiddle, ge, go, vg, v):
+    T, D = x.shape
+    FF = ge.shape[1]
+    R, Q, pairs = D // 8, FF // 4, H // 2
+    vm = pltpu.VMEM
+    n = 12 + 12 + 6 * 12 + 60 + 6
     return pl.pallas_call(
-        back_kernel, in_specs=[pl.BlockSpec(memory_space=pltpu.SMEM), V, V, V, V], out_specs=V,
-        out_shape=jax.ShapeDtypeStruct((T, 3 * D), BF),
-        scratch_shapes=[pltpu.VMEM((2, T, 128), BF), pltpu.VMEM((2, T, 128), BF), pltpu.VMEM((2, 128, T), F32),
-                        pltpu.VMEM((2, T, 128), BF), pltpu.VMEM((2, 128, T), BF)],
-        compiler_params=pltpu.CompilerParams(vmem_limit_bytes=60 << 20), name="back_part")(
-            length, proj, mixed, qa, dm)
+        third_kernel,
+        in_specs=[SM] + [ANY] * 10 + [VM] * 2,
+        out_specs=[ANY] + [VM] * 4,
+        out_shape=[sds((T, D), BF), sds((R, 3 * D // 4), F32), sds((R, D // 4), F32), sds((R, Q), F32),
+                   sds((3, 8, 384), F32)],
+        scratch_shapes=[
+            vm((T, 3 * D), BF), vm((H, T, 128), BF), vm((T, D), BF), vm((T, D), BF), vm((T, D), BF), vm((D, T), BF),
+            vm((D, 3 * D), BF), vm((T, D), BF), vm((T, D), F32), vm((D, FF), BF), vm((8, 4, R, 256), BF),
+            vm((T, 3 * D), BF), vm((T, D), BF), vm((pairs, 8, R, 384), BF),
+            vm((2, T, 128), BF), vm((2, T, 128), BF), vm((2, 128, T), F32), vm((2, T, 128), BF), vm((2, 128, T), BF),
+            vm((16, D), F32), vm((9, 16, D), F32),
+            vm((4, R, FF), BF), vm((R, FF // 2), BF), vm((R, FF // 2), BF), vm((R, FF), BF), vm((R, FF), BF), vm((4, R, Q), BF),
+            vm((4, 4, R, 256), BF), vm((2, R, 256), BF), vm((2, R, 256), BF), vm((4, R, 256), BF), vm((4, R, 256), BF),
+            vm((4, R, 256), BF),
+            vm((pairs, 4, R, 384), BF), vm((pairs, R // 2, 384), BF), vm((pairs, R // 2, 384), BF),
+            vm((pairs, R, 384), BF), vm((pairs, R, 384), BF), vm((20, 3, R, 128), BF), vm((R, 640), F32),
+            pltpu.SemaphoreType.DMA((n,)), pltpu.SemaphoreType.DMA((n,)), pltpu.SemaphoreType.DMA((28,)),
+        ],
+        compiler_params=pltpu.CompilerParams(
+            collective_id=2, has_side_effects=True, vmem_limit_bytes=63 << 20),
+        name="third_part",
+    )(length, proj, qa, mixed, dm, n1, wp, x, dmiddle, ge, go, vg, v)
 
 
 def per_device_fast(tokens, lengths, cotangent, project_weight, project_bias, output_weight, output_bias,
                     expand_weight, expand_bias, contract_weight, contract_bias, first_gain, first_shift,
                     second_gain, second_shift):
-    T, D = tokens.shape
-    wide = lax.all_gather(contract_weight, "fsdp", axis=1, tiled=True)
-    full_contract = lax.all_gather(wide, "dp", axis=0, tiled=True)
     vec = pack_vectors(project_bias, output_bias, expand_bias, contract_bias,
                        first_gain, first_shift, second_gain, second_shift)
-    normed_one, projected, mixed_low, qa, full_project, full_output, full_expand, v = first_call(
+    normed_one, projected, mixed, qa, full_project, full_output, full_expand, v = first_call(
         lengths, tokens, project_weight, output_weight, expand_weight, vec)
-    bias_expand = v[1]
-    bias_output, bias_contract, gain_one, shift_one, gain_two, shift_two = [v[i, :D] for i in range(2, 8)]
-    live = (jnp.arange(T) < lengths[0])[:, None]
-    rows_in = tokens.astype(F32)
-    middle = rows_in + (matmul(mixed_low, full_output) + bias_output)
-    normed_two = layer_norm(middle, gain_two, shift_two).astype(BF)
-    hidden = matmul(normed_two, full_expand) + bias_expand
-    active = gelu_exact(hidden).astype(BF)
-    result = middle + (matmul(active, full_contract) + bias_contract)
-    block_out = jnp.where(live, result, 0.0).astype(BF)
-    grad_out = jnp.where(live, cotangent.astype(F32), 0.0)
-    grad_out_low = grad_out.astype(BF)
-    grad_contract = over_rows(active, grad_out_low)
-    grad_contract_bias = jnp.sum(grad_out, axis=0)
-    grad_active = over_columns(grad_out_low, full_contract)
-    gelu_value, gelu_pull = jax.vjp(gelu_exact, hidden)
-    grad_hidden = gelu_pull(grad_active)[0].astype(BF)
-    grad_expand = over_rows(normed_two, grad_hidden)
-    grad_expand_bias = jnp.sum(grad_hidden.astype(F32), axis=0)
-    grad_normed_two = over_columns(grad_hidden, full_expand)
-    norm_value, second_pull = jax.vjp(layer_norm, middle, gain_two, shift_two)
-    grad_middle, grad_gain_two, grad_shift_two = second_pull(grad_normed_two)
-    grad_middle = grad_middle + grad_out
-    grad_branch = grad_middle.astype(BF)
-    grad_output = over_rows(mixed_low, grad_branch)
-    grad_output_bias = jnp.sum(grad_branch.astype(F32), axis=0)
-    grad_mixed = over_columns(grad_branch, full_output).astype(BF)
-    grad_projected = back_call(lengths, projected, mixed_low, qa, grad_mixed)
-    grad_project = over_rows(normed_one, grad_projected)
-    column_sums = jnp.sum(grad_projected.astype(F32), axis=0)
-    grad_project_bias = jnp.concatenate([column_sums[:D], column_sums[2 * D:]])
-    grad_normed_one = over_columns(grad_projected, full_project)
-    first_value, first_pull = jax.vjp(layer_norm, rows_in, gain_one, shift_one)
-    grad_rows_in, grad_gain_one, grad_shift_one = first_pull(grad_normed_one)
-    tokens_grad = (grad_rows_in + grad_middle).astype(BF)
-
-    def scatter(g):
-        g = lax.psum_scatter(g.astype(BF), "dp", scatter_dimension=0, tiled=True)
-        return lax.psum_scatter(g, "fsdp", scatter_dimension=1, tiled=True).astype(F32)
-
-    small = (grad_project_bias, grad_output_bias, grad_expand_bias, grad_contract_bias,
-             grad_gain_one, grad_shift_one, grad_gain_two, grad_shift_two)
-    total = lax.psum(jnp.concatenate(small), ("dp", "fsdp"))
-    d = lax.axis_index("dp")
-    picked, at = [], 0
-    for item in small:
-        n = item.shape[0]
-        picked.append(lax.dynamic_slice(total, (at + d * (n // 8),), (n // 8,)))
-        at += n
-    return (block_out, tokens_grad, scatter(grad_project), picked[0], scatter(grad_output), picked[1],
-            scatter(grad_expand), picked[2], scatter(grad_contract), picked[3],
-            picked[4], picked[5], picked[6], picked[7])
+    block_out, grad_mixed, grad_middle, ge, go, grad_contract, vg = second_call(
+        lengths, tokens, cotangent, mixed, full_output, full_expand, contract_weight, v)
+    tokens_grad, grad_project, grad_output, grad_expand, vo = third_call(
+        lengths, projected, qa, mixed, grad_mixed, normed_one, full_project, tokens, grad_middle, ge, go, vg, v)
+    r = output_bias.shape[0]
+    return (block_out, tokens_grad, grad_project, vo[1, 0, :2 * r], grad_output, vo[0, 0, :r],
+            grad_expand, vo[2, 0, :4 * r], grad_contract, vo[0, 1, :r],
+            vo[0, 2, :r], vo[0, 3, :r], vo[0, 4, :r], vo[0, 5, :r])
 
 
 def solution(mesh):

time: 500 us -> 295 us (0.59); the launches traced: 494 us -> 294 us
  Pallas kernels: 145 us -> 274 us
  matrix products: 122 us -> 0 us
  waiting for transfers between devices: 92.2 us -> 0 us
  blocking collectives: 60.7 us -> 0 us
  local copies, waits for them, and re-layouts: 40 us -> 18.6 us
  other arithmetic: 17.7 us -> 0 us
  between operations: 15.4 us -> 1.35 us
    pallas_call x1 -> x2, Pallas kernels: 47.7 us -> 181 us  [the longest x1 104 us: third_call(): pl.pallas_call(third_kernel, in_specs=[SM] + [ANY] * 10 + [VM] * 2, out_s...]
    dot_general x11 -> x0, matrix products: 122 us -> none  [the longest x3 49.4 us: matmul(): return jnp.dot(first, second, preferred_element_type=jnp.float32)]
    reduce_scatter x5 -> x0, waiting for transfers between devices: 61.5 us -> none  [the longest x4 40.5 us: scatter(): g = lax.psum_scatter(g.astype(BF), 'dp', scatter_dimension=0, tiled=True)]
    psum x1 -> x0, blocking collectives: 40.4 us -> none  [per_device_fast(): total = lax.psum(jnp.concatenate(small), ('dp', 'fsdp'))]
    unnamed x12 -> x0, waiting for transfers between devices: 30.7 us -> none
    all_gather x1 -> x0, blocking collectives: 20.3 us -> none  [per_device_fast(): wide = lax.all_gather(contract_weight, 'fsdp', axis=1, tiled=True)]
    unnamed x59 -> x17, local copies, waits for them, and re-layouts: 23.4 us -> 8.57 us
    reduce_sum x9 -> x0, other arithmetic: 14.7 us -> none  [the longest x2 4.28 us: layer_norm(): return centred * lax.rsqrt(spread + eps_norm) * gain_row + shift_row]
  transfers between devices with their start and end apart: 9 -> 0, of which waited for: 5 -> 0; matrix products, arithmetic and copies ran while one was open for 35% -> 0% of each run, Pallas kernels for 29% -> 0%
where the time goes in v2:
time: 295 us; the launch traced here: 294 us
  Pallas kernels  274 us (93%)
  local copies, waits for them, and re-layouts  18.6 us (6%)
    pallas_call x1, Pallas kernels, third_call(): pl.pallas_call(third_kernel, in_specs=[SM] + [ANY] * 10 + [VM] * 2, out_s...  104 us
    pallas_call x1, Pallas kernels, first_call(): pl.pallas_call(first_kernel, in_specs=[S, V, V, V, V, V], out_specs=[ANY]...  93.6 us
    pallas_call x1, Pallas kernels, second_call(): pl.pallas_call(second_kernel, in_specs=[SM, VM, VM, VM, VM, ANY, VM, VM],...  76.8 us
    unnamed x17, local copies, waits for them, and re-layouts  8.57 us

profile of v2, /device:TPU:0, one launch (start us, length us, event | category | flops | bytes accessed | tf_op | source)
XLA Modules:
  0.0 294.2 jit_solution(15068745691156549411)
XLA Ops:
  1.3 0.7 pad.27
  2.0 0.7 pad.28
  2.6 0.7 pad.29
  3.3 0.7 pad.30
  4.0 0.7 pad.31
  4.6 0.7 pad.32
  5.3 0.7 pad.33
  6.0 0.7 stack.29
  6.7 0.6 pad.34.vec_ref
  7.3 1.7 copy.29.wc_ref
  9.0 93.6 %first_part.1 = (bf16[1024,768]{1,0:T(8,128)(2,1)}, bf16[1024,2304]{1,0:T(8,128)(2,1)}, bf16[1024,768]{1,0:T(8,128)(2,1)}, bf16[12,1024,128]{2,1,0:T(8,128)(2,1)...) custom-call(s32[1]{0:T(128)S(6)} %copy.36.length_ref, ...), custom_call_target="tpu_custom_call" | custom-call | tf_op jit(solution)/shard_map/first_part/pallas_call | solution.py:376
  102.6 76.8 %second_part.1 = (bf16[1024,768]{1,0:T(8,128)(2,1)}, bf16[1024,768]{1,0:T(8,128)(2,1)}, f32[1024,768]{1,0:T(8,128)}, bf16[768,3072]{1,0:T(8,128)(2,1)}, bf16[8,4...) custom-call(s32[1]{0:T(128)S(6)} %copy.36.length_ref, bf16[1024,768]{1,0:T(8,128)(2,1)} %x_hbm.1, ...), custom_call_target="tpu_custom_call" | custom-call | tf_op jit(solution)/shard_map/second_part/pallas_call | solution.py:979
  179.4 0.0 copy-start.1
  179.4 103.9 %third_part.1 = (bf16[1024,768]{1,0:T(8,128)(2,1)}, f32[96,576]{1,0:T(8,128)}, f32[96,192]{1,0:T(8,128)}, f32[96,768]{1,0:T(8,128)}, f32[3,8,384]{2,1,0:T(8,128)}) custom-call(s32[1]{0:T(128)S(6)} %copy.36.length_ref, bf16[1024,2304]{1,0:T(8,128)(2,1)} %get-tuple-element.39.proj_hbm, bf16[12,1024,128]{2,1,0:T(8,128)(2,1)} %get-tuple-element.40.qa_hbm, ...), custom_call_target="tpu_custom_call" | custom-call | tf_op jit(solution)/shard_map/third_part/pallas_call | solution.py:1260
  283.4 1.3 slice.24
  284.6 1.3 slice_reduce_fusion
  285.9 1.4 slice_bitcast_fusion
  287.4 0.0 copy-done.1
  287.4 0.9 copy.30
  288.2 0.0 copy-start
  288.2 2.8 copy.37
  291.0 0.0 copy-done
  291.0 0.0 copy-start.3
  291.0 0.0 copy-start.4
  291.0 0.0 copy-start.2
  291.0 1.1 copy.38
  292.2 0.0 copy-done.3
  292.2 0.7 copy.39
  292.9 0.0 copy-done.4
  292.9 0.6 copy.40
  293.5 0.0 copy-done.2
  293.5 0.7 copy.41
  (8 shorter events, 0.1 us)
Async XLA Ops:
  179.4 107.9 %copy-start.1 = (f32[384,192]{1,0:T(8,128)S(1)}, f32[384,192]{1,0:T(8,128)}, u32[]{:S(2)}) copy-start(f32[384,192]{1,0:T(8,128)} %get-tuple-element.62) | copy-start | bytes 884740
  288.2 2.8 copy-start
  291.0 1.2 copy-start.3
  291.0 1.9 copy-start.4
  291.0 2.5 copy-start.2

commit v3 on v2

--- a/solution.py
+++ b/solution.py
@@ -43,6 +43,9 @@
         self.dy = self.d + 4 - 8 * up
         self.dd = self.dx + 4 - 8 * up
         self.odd = lax.rem(self.z, 2)
+        z = self.z
+        pick = lambda a, b, c, d: jnp.where(z < 2, jnp.where(z == 0, a, b), jnp.where(z == 2, c, d))
+        self.order = [z, pick(1, 0, 3, 2), pick(2, 2, 1, 1), pick(3, 3, 0, 0)]
 
     def zt(self, step):
         return lax.rem(self.z + step, 4)
@@ -75,91 +78,124 @@
         self.count = 0
         self.copies = []
 
-    def slot(self):
-        self.count += 1
-        return self.count - 1
-
-    def copy(self, slot, source, target, to):
+    def slot(self, many=1):
+        self.count += many
+        return self.count - many
+
+    def copy(self, slot, source, target, to, land=None):
         return pltpu.make_async_remote_copy(
             src_ref=source, dst_ref=target, send_sem=self.send_sem.at[slot],
-            recv_sem=self.recv_sem.at[slot], device_id=self.place.id(to), device_id_type=MESH)
-
-    def send(self, slot, source, target, to, like):
-        self.copy(slot, source, target, to).start()
-        self.copies.append((slot, like))
+            recv_sem=self.recv_sem.at[slot if land is None else land], device_id=self.place.id(to),
+            device_id_type=MESH)
+
+    def send(self, slot, source, target, to, like, land=None, when=None):
+        def start():
+            self.copy(slot, source, target, to, land).start()
+
+        if when is None:
+            start()
+        else:
+            pl.when(when())(start)
+        self.copies.append((slot, like, when))
 
     def got(self, slot, target):
         self.copy(slot, target, target, "x").wait_recv()
 
     def finish(self):
-        for slot, like in self.copies:
-            view = like()
-            self.copy(slot, view, view, "x").wait_send()
-
-
-def gather_events(link, place, block):
+        for slot, like, when in self.copies:
+            def done(slot=slot, like=like):
+                view = like()
+                self.copy(slot, view, view, "x").wait_send()
+
+            if when is None:
+                done()
+            else:
+                pl.when(when())(done)
+
+
+class Gather:
+    def __init__(self, link, place, block):
+        p = place
+        zr, zs = link.slot(4), link.slot(5)
+        xs, ys, fx = link.slot(4), link.slot(4), link.slot(4)
+        cs = link.slot(16)
+        got = link.got
+        send = functools.partial(link.send, like=lambda: block(0, 0))
+        inner = lambda: (p.z == 1) | (p.z == 2)
+
+        def z_step(a):
+            def run():
+                b = p.order[a]
+                here = block(b, p.d)
+                if a == 0:
+                    send(zs, here, here, ("z", p.z + 1), land=zr + p.z, when=lambda: p.z < 3)
+                    send(zs + 1, here, here, ("z", p.z - 1), land=zr + p.z, when=lambda: p.z > 0)
+                else:
+                    got(zr + b, here)
+                    to = jnp.where(b < p.z, p.z + 1, p.z - 1)
+                    send(zs + 1 + a, here, here, ("z", to), land=zr + b, when=inner)
+            return run
+
+        def x_step(a):
+            def run():
+                here = block(p.order[a], p.d)
+                send(xs + a, here, here, "x")
+                send(ys + a, here, here, "y")
+                send(cs + a, here, here, "c")
+            return run
+
+        def turn(a):
+            def run():
+                b = p.order[a]
+                bx, by = block(b, p.dx), block(b, p.dy)
+                got(xs + a, bx)
+                got(ys + a, by)
+                if a in (0, 1):
+                    send(fx + a, bx, bx, "y")
+                else:
+                    send(fx + a, by, by, "x")
+                send(cs + 4 + a, bx, bx, "c")
+                send(cs + 8 + a, by, by, "c")
+            return run
+
+        def corner(a):
+            def run():
+                bd = block(p.order[a], p.dd)
+                got(fx + a, bd)
+                send(cs + 12 + a, bd, bd, "c")
+            return run
+
+        def close():
+            sib = p.dc - p.d
+            for which, d in enumerate((p.d, p.dx, p.dy, p.dd)):
+                for a in range(4):
+                    got(cs + 4 * which + a, block(p.order[a], d + sib))
+
+        self.z, self.x, self.t, self.q = ([make(a) for a in range(4)] for make in (z_step, x_step, turn, corner))
+        self.close = close
+
+
+def spread_z(link, place, ref):
     p = place
-    zs = [link.slot() for _ in range(4)]
-    xs = [link.slot() for _ in range(4)]
-    ys = [link.slot() for _ in range(4)]
-    fx = [link.slot() for _ in range(4)]
-    cs = [[link.slot() for _ in range(4)] for _ in range(4)]
-    got = link.got
-    send = functools.partial(link.send, like=lambda: block(0, 0))
-
-    def begin():
-        own = block(p.z, p.d)
+    zs, zr = link.slot(3), link.slot(4)
+
+    def send():
         for step in (1, 3, 2):
-            send(zs[step], own, own, step)
-        for slots, to in ((xs, "x"), (ys, "y")):
-            send(slots[0], own, own, to)
-        send(cs[0][0], own, own, "c")
-
-    def onward(step):
-        def run():
-            here = block(p.zf(step), p.d)
-            got(zs[step], here)
-            for slots, to in ((xs, "x"), (ys, "y")):
-                send(slots[step], here, here, to)
-            send(cs[0][step], here, here, "c")
-        return run
-
-    def turn(step):
-        def run():
-            z = p.zf(step)
-            bx, by = block(z, p.dx), block(z, p.dy)
-            got(xs[step], bx)
-            got(ys[step], by)
-            if step in (0, 1):
-                send(fx[step], bx, bx, "y")
-            else:
-                send(fx[step], by, by, "x")
-            send(cs[1][step], bx, bx, "c")
-            send(cs[2][step], by, by, "c")
-        return run
-
-    def corner(step):
-        def run():
-            z = p.zf(step)
-            bd = block(z, p.dd)
-            got(fx[step], bd)
-            send(cs[3][step], bd, bd, "c")
-        return run
-
-    def close():
-        dc = p.dc
-        core = lax.rem(dc, 2)
-        across = lax.rem(lax.div(dc, 2), 2)
-        up = lax.div(dc, 4)
-        cx = dc + 2 - 4 * across
-        cy = dc + 4 - 8 * up
-        cd = cx + 4 - 8 * up
-        for which, d in enumerate((dc, cx, cy, cd)):
-            for step in range(4):
-                got(cs[which][step], block(p.zf(step), d))
-
-    return ([begin, onward(1), onward(3), turn(0), onward(2), turn(1), turn(3), turn(2)]
-            + [corner(0), corner(1), corner(3), corner(2), close])
+            link.send(zs + step - 1, ref.at[p.z], ref.at[p.z], step, lambda: ref.at[0], land=zr + p.z)
+
+    def wait():
+        for step in range(1, 4):
+            b = p.zf(step)
+            link.got(zr + b, ref.at[b])
+
+    return send, wait
+
+
+def run(*events):
+    def together():
+        for event in events:
+            event()
+    return together
 
 
 def window(value, odd, wide):
@@ -212,9 +248,14 @@
 QB = 512
 
 
-def first_kernel(length_ref, x_ref, wp_ref, wo_ref, we_ref, vec_ref,
-                 n1_out, proj_out, mixed_out, qa_out, wp_out, wo_out, we_out, v_out,
-                 wp_blk, wo_blk, we, wp, wo, vb, n1, proj, mixed, qa, ka, va, vrow,
+def first_kernel(length_ref, x_ref, wp_ref, wo_ref, we_ref, wc_ref, *refs):
+    vec_refs, refs = refs[:8], refs[8:]
+    first_body(length_ref, x_ref, wp_ref, wo_ref, we_ref, wc_ref, vec_refs, *refs)
+
+
+def first_body(length_ref, x_ref, wp_ref, wo_ref, we_ref, wc_ref, vec_refs,
+                 n1_out, proj_out, mixed_out, qa_out, wp_out, wo_out, we_out, c_out, v_out,
+                 wp_blk, wo_blk, we, wp, wo, vb, n1, proj, mixed, qa, ka, va, vrow, cc,
                  send_sem, recv_sem, out_sem):
     p = Place()
     T, D = x_ref.shape
@@ -225,13 +266,16 @@
     bp = lambda z, d: wp_blk.at[z, rows_of(d), :]
     bo = lambda z, d: wo_blk.at[z, rows_of(d), :]
     be = lambda z, d: we.at[rows_of(d), pl.ds(mo(z * (FF // 4), 128), FF // 4)]
-    ev_p, ev_o, ev_e = (gather_events(link, p, b) for b in (bp, bo, be))
+    gp, go, ge = (Gather(link, p, b) for b in (bp, bo, be))
+    c_send, c_wait = spread_z(link, p, cc)
     vs = [link.slot() for _ in range(7)]
 
     wp_blk[p.z, rows_of(p.d), :] = window(wp_ref[...], p.odd, wp_blk.shape[2])
     wo_blk[p.z, rows_of(p.d), :] = window(wo_ref[...], p.odd, wo_blk.shape[2])
     we[rows_of(p.d), pl.ds(mo(p.z * (FF // 4), 128), FF // 4)] = we_ref[...]
-    vb[p.d] = vec_ref[...]
+    cc[p.z] = wc_ref[...]
+    for i, ref in enumerate(vec_refs):
+        vb[p.d, i:i + 1, 0:ref.shape[0]] = ref[...].astype(F32).reshape(1, ref.shape[0]).astype(BF)
 
     outs = []
 
@@ -244,26 +288,18 @@
     send_v = lambda slot, d, to: link.send(vs[slot], vb.at[d], vb.at[d], to, lambda: vb.at[0])
     for slot, to in ((0, "x"), (1, "y"), (3, "c")):
         send_v(slot, p.d, to)
-    ev_p[0]()
+    run(gp.z[0], gp.x[0])()
     link.got(vs[0], vb.at[p.dx])
     link.got(vs[1], vb.at[p.dy])
     send_v(2, p.dx, "y")
     send_v(4, p.dx, "c")
     send_v(5, p.dy, "c")
-    ev_p[1]()
-    ev_p[2]()
+    run(gp.z[1], gp.x[1], gp.t[0], gp.z[2], gp.x[2])()
     link.got(vs[2], vb.at[p.dd])
     send_v(6, p.dd, "c")
-    ev_p[3]()
-    ev_p[4]()
-    dc = p.dc
-    link.got(vs[3], vb.at[dc])
-    cx = p.dx + p.dc - p.d
-    cy = p.dy + p.dc - p.d
-    cd = p.dd + p.dc - p.d
-    link.got(vs[4], vb.at[cx])
-    link.got(vs[5], vb.at[cy])
-    link.got(vs[6], vb.at[cd])
+    sib = p.dc - p.d
+    for slot, d in ((3, p.d), (4, p.dx), (5, p.dy), (6, p.dd)):
+        link.got(vs[slot], vb.at[d + sib])
     got = vb[...].astype(F32)
     side = lambda row, wide: jnp.concatenate([got[i, row:row + 1, 0:wide] for i in range(8)], axis=1)
     bias = side(0, 2 * R)
@@ -274,7 +310,7 @@
     for row, at in ((2, 1), (3, 3), (4, 4), (5, 5), (6, 6), (7, 7)):
         vrow[row:row + 1, 0:D] = side(at, R)
     out(vrow, v_out)
-    ev_p[5]()
+    run(gp.t[1], gp.z[3], gp.x[3], ge.z[0], go.z[0])()
 
     LR = 128
     gain, shift = vrow[4:5, 0:D], vrow[5:6, 0:D]
@@ -287,17 +323,22 @@
         n1[r, :] = (u * lax.rsqrt(spread + eps_norm) * gain + shift).astype(BF)
         return 0
 
-    lax.fori_loop(0, T // LR, norm_body, 0)
+    norm_part = lambda k: lax.fori_loop(k * (T // LR // 4), (k + 1) * (T // LR // 4), norm_body, 0)
+    norm_part(0)
+    gp.t[2]()
+    norm_part(1)
+    gp.t[3]()
+    norm_part(2)
+    run(ge.x[0], go.x[0], gp.q[0])()
+    norm_part(3)
     out(n1, n1_out)
-    for event in ev_p[6:]:
-        event()
-    ev_o[0]()
+    run(gp.q[1], gp.q[2], ge.z[1], ge.x[1], gp.q[3], gp.close, go.z[1], go.x[1])()
     merge_windows(wp_blk, wp, 9, 96)
     out(wp, wp_out)
-    ev_o[1]()
-    ev_o[2]()
 
     def project_body(i, _):
+        for at, event in ((1, run(ge.z[2], ge.x[2])), (2, run(ge.t[0], go.t[0])), (3, run(go.z[2], go.x[2]))):
+            pl.when(i == at)(event)
         r = pl.ds(mo(i * 256, 256), 256)
         left = n1[r, :]
         for j in range(3):
@@ -351,10 +392,11 @@
 
         lax.fori_loop(0, (H // 2) * nq, body, 0)
 
-    rest = ev_o[3:] + ev_e
-    spots = [0, 0, 0, 0, 1, 1, 1, 1, 1, 1] + [2, 3, 3, 4, 4, 5, 5, 6, 7, 8, 8, 9, 10]
-    assert len(rest) == len(spots)
-    attend_steps(list(zip(spots, rest)))
+    attend_steps([(1, run(ge.t[1], go.t[1])), (2, run(ge.z[3], ge.x[3], go.z[3], go.x[3], c_send)),
+                  (3, run(ge.t[2], ge.q[0])), (4, run(go.t[2], go.q[0])), (6, run(ge.q[1], go.q[1])), (7, ge.q[2]),
+                  (8, run(ge.t[3], go.t[3], go.q[2])), (11, ge.q[3])])
+    run(go.q[3], c_wait, ge.close, go.close)()
+    out(cc, c_out)
     merge_windows(wo_blk, wo, 3, 96)
     out(wo, wo_out)
     out(we, we_out)
@@ -365,39 +407,32 @@
         made.wait()
 
 
-def first_call(length, x, wp, wo, we, vec):
+def first_call(length, x, wp, wo, we, wc, vectors):
     T, D = x.shape
     FF = we.shape[1] * 4
     ANY = pl.BlockSpec(memory_space=pl.ANY)
     V = pl.BlockSpec(memory_space=pltpu.VMEM)
     S = pl.BlockSpec(memory_space=pltpu.SMEM)
     sds = jax.ShapeDtypeStruct
-    n = 3 * 32 + 7
+    n = 3 * 37 + 7 + 7
     return pl.pallas_call(
         first_kernel,
-        in_specs=[S, V, V, V, V, V],
-        out_specs=[ANY] * 8,
+        in_specs=[S] + [V] * 13,
+        out_specs=[ANY] * 9,
         out_shape=[sds((T, D), BF), sds((T, 3 * D), BF), sds((T, D), BF), sds((H, T, 128), BF),
-                   sds((D, 3 * D), BF), sds((D, D), BF), sds((D, FF), BF), sds((8, FF), F32)],
+                   sds((D, 3 * D), BF), sds((D, D), BF), sds((D, FF), BF), sds((4,) + wc.shape, BF), sds((8, FF), F32)],
         scratch_shapes=[
             pltpu.VMEM((4, D, 640), BF), pltpu.VMEM((4, D, 256), BF), pltpu.VMEM((D, FF), BF),
-            pltpu.VMEM((D, 3 * D), BF), pltpu.VMEM((D, D), BF), pltpu.VMEM((8,) + vec.shape, BF),
+            pltpu.VMEM((D, 3 * D), BF), pltpu.VMEM((D, D), BF), pltpu.VMEM((8, 16, FF // 8), BF),
             pltpu.VMEM((T, D), BF), pltpu.VMEM((T, 3 * D), BF), pltpu.VMEM((T, D), BF),
             pltpu.VMEM((H, T, 128), BF), pltpu.VMEM((2, T, 128), BF), pltpu.VMEM((2, T, 128), BF),
-            pltpu.VMEM((8, FF), F32),
-            pltpu.SemaphoreType.DMA((n,)), pltpu.SemaphoreType.DMA((n,)), pltpu.SemaphoreType.DMA((8,)),
+            pltpu.VMEM((8, FF), F32), pltpu.VMEM((4,) + wc.shape, BF),
+            pltpu.SemaphoreType.DMA((n,)), pltpu.SemaphoreType.DMA((n,)), pltpu.SemaphoreType.DMA((9,)),
         ],
         compiler_params=pltpu.CompilerParams(
             collective_id=0, has_side_effects=True, vmem_limit_bytes=60 << 20),
         name="first_part",
-    )(length, x, wp, wo, we, vec)
-
-
-def pack_vectors(project_bias, output_bias, expand_bias, contract_bias, g1, s1, g2, s2):
-    wide = expand_bias.shape[0]
-    rows = [jnp.pad(v, (0, wide - v.shape[0])) for v in
-            (project_bias, output_bias, expand_bias, contract_bias, g1, s1, g2, s2)]
-    return jnp.pad(jnp.stack(rows), ((0, 8), (0, 0)))
+    )(length, x, wp, wo, we, wc, *vectors)
 
 
 def layer_norm(values, gain_row, shift_row):
@@ -747,12 +782,11 @@
     )
 
 
-def scatter_events(link, place, col, pair_of, block_of, lc, lxh, lyh, lx, ly, lz, finish):
+def scatter_events(link, place, col, pair_of, lc, lxh, lyh, lx, ly):
     p = place
     family = (p.dc, p.dx + p.dc - p.d, p.dy + p.dc - p.d, p.dd + p.dc - p.d)
     cs = [link.slot() for _ in range(4)]
     hx, hy, fx, fy = (link.slot() for _ in range(4))
-    zs = [link.slot() for _ in range(4)]
     got = link.got
 
     def add(target, *terms):
@@ -789,21 +823,30 @@
     def own():
         got(cs[0], lc.at[0])
 
-    def along_z():
+    def total():
         got(fx, lx)
         got(fy, ly)
         add(col(p.d), lc.at[0], lx, ly)
-        for step in (1, 3, 2) if lz is not None else ():
-            link.send(zs[step], block_of(col(p.d), p.zt(step)), lz.at[step], step, lambda: lz.at[0])
+
+    return to_sibling, [halves, near, pass_y, pass_x, own, total]
+
+
+def z_sum(link, place, block, lz, finish):
+    p = place
+    zs = link.slot(4)
+
+    def send():
+        for step in (1, 3, 2):
+            link.send(zs + step, block(p.zt(step)), lz.at[step], step, lambda: lz.at[0])
 
     def last():
-        total = block_of(col(p.d), p.z)[...].astype(F32)
+        total = block(p.z)[...].astype(F32)
         for step in (1, 3, 2):
-            got(zs[step], lz.at[step])
+            link.got(zs + step, lz.at[step])
             total = total + lz[step].astype(F32)
         finish(total)
 
-    return to_sibling, [halves, near, pass_y, pass_x, own, along_z, last]
+    return send, last
 
 
 def gelu_pair(value):
@@ -812,10 +855,10 @@
     return value * lift, lift + value * bell
 
 
-def second_kernel(length_ref, x_ref, cot_ref, mixed_ref, wo_ref, we_hbm, wc_ref, v_ref,
+def second_kernel(length_ref, x_ref, cot_ref, mixed_ref, wo_ref, we_hbm, c_hbm, v_ref,
                   block_out, dmixed_out, dmiddle_out, ge_out, go_out, gc_out, vg_out,
                   we, wct, act, slope, middle, n2t, dot_t, mixed_t, dbranch, dout, gc, go, dmixed, bout, vg,
-                  lc, lxh, lyh, lx, ly, lz, send_sem, recv_sem, out_sem):
+                  lc, lxh, lyh, lx, ly, send_sem, recv_sem, out_sem):
     p = Place()
     T, D = x_ref.shape
     FF = we.shape[1]
@@ -824,19 +867,19 @@
     C8 = FF // 8
     link = Link(p, send_sem, recv_sem)
     bc = lambda z, d: wct.at[pl.ds(mo(z * (D // 4), 16), D // 4), pl.ds(mo(d * C8, 128), C8)]
-    gather = gather_events(link, p, bc)
-
-    def finish(total):
-        gc_out[...] = total.T
+    gather = Gather(link, p, bc)
 
     to_sibling, scatter = scatter_events(
-        link, p, lambda d: gc.at[d], lambda ref, h: ref.at[pl.ds(2 * h, 2)], lambda ref, z: ref.at[z],
-        lc, lxh, lyh, lx, ly, lz, finish)
+        link, p, lambda d: gc.at[d], lambda ref, h: ref.at[pl.ds(2 * h, 2)], lc, lxh, lyh, lx, ly)
     load = pltpu.make_async_copy(we_hbm, we, out_sem.at[0])
+    columns = [pltpu.make_async_copy(c_hbm.at[z], bc(z, p.d), out_sem.at[8 + z]) for z in range(4)]
+    for made in columns:
+        made.start()
     load.start()
-    wct[pl.ds(mo(p.z * (D // 4), 16), D // 4), pl.ds(mo(p.d * C8, 128), C8)] = wc_ref[...].astype(F32).T.astype(BF)
     enter(p)
-    gather[0]()
+    for made in columns:
+        made.wait()
+    run(*gather.x)()
     length = length_ref[0]
     LR = 256
     rows = lambda i: pl.ds(mo(i * LR, LR), LR)
@@ -853,7 +896,7 @@
         return u * r, r
 
     def middle_body(i, _):
-        at(i, [(1, gather[1]), (3, gather[2])])
+        at(i, [(3, gather.t[0])])
         r = rows(i)
         value = x_ref[r, :].astype(F32) + (dot(mixed_ref[r, :], wo_ref[...]) + vec(2))
         middle[r, :] = value
@@ -873,8 +916,7 @@
     load.wait()
 
     def hidden_body(i, _):
-        at(i, [(0, gather[3]), (1, gather[4]), (1, gather[5]), (2, gather[6]), (2, gather[7]), (3, gather[8]),
-               (3, gather[9])])
+        at(i, [(1, gather.t[1]), (2, gather.t[2]), (3, run(gather.t[3], gather.q[0]))])
         r = rows(i)
         left = dmixed[r, :]
         for j in range(4):
@@ -885,7 +927,6 @@
         return 0
 
     lax.fori_loop(0, T // LR, hidden_body, 0)
-    gather[10]()
 
     def column(d):
         value = dot(dot_t[...], act[:, pl.ds(mo(d * C8, 128), C8)])
@@ -895,22 +936,23 @@
     column(p.dd + sib)
     to_sibling(3)
     column(p.dd)
-    gather[11]()
+    gather.q[1]()
     column(p.dx + sib)
     to_sibling(1)
     column(p.dy + sib)
     to_sibling(2)
+    gather.q[2]()
+    column(p.dx)
     scatter[0]()
-    column(p.dx)
     column(p.dy)
-    scatter[1]()
+    gather.q[3]()
     column(p.d + sib)
     to_sibling(0)
     column(p.d)
-    gather[12]()
+    run(scatter[1], gather.close)()
 
     def back_body(i, _):
-        at(i, [(0, scatter[2]), (0, scatter[3]), (1, scatter[4]), (3, scatter[5])])
+        at(i, [(1, run(scatter[2], scatter[3], scatter[4]))])
         r = rows(i)
         grad_low = dout[r, :]
         result = middle[r, :] + vec(3)
@@ -953,12 +995,13 @@
     for z in range(4):
         act[0:D, z * Q:(z + 1) * Q] = dot(n2t[...], slope[:, z * Q:(z + 1) * Q]).astype(BF)
     out(act.at[0:D, :], ge_out)
+    scatter[5]()
+    out(gc.at[p.d], gc_out)
     for z in range(4):
         cols = slice(3 * z // 2 * 128, 3 * z // 2 * 128 + 256)
         go[:, z] = dot(mixed_t[...], dbranch[:, cols]).reshape(8, R, 256).astype(BF)
     out(go, go_out)
     vg_out[...] = vg[...]
-    scatter[6]()
     link.finish()
     for made in outs:
         made.wait()
@@ -973,22 +1016,21 @@
 def second_call(length, x, cot, mixed, wo, we, wc, v):
     T, D = x.shape
     FF = we.shape[1]
-    n = 32 + 12
+    n = 37 + 8
     R, C8, Z = D // 8, FF // 8, D // 4
     vm = pltpu.VMEM
     return pl.pallas_call(
         second_kernel,
-        in_specs=[SM, VM, VM, VM, VM, ANY, VM, VM],
-        out_specs=[ANY] * 5 + [VM] * 2,
+        in_specs=[SM, VM, VM, VM, VM, ANY, ANY, VM],
+        out_specs=[ANY] * 6 + [VM],
         out_shape=[sds((T, D), BF), sds((T, D), BF), sds((T, D), F32), sds((D, FF), BF), sds((8, 4, R, 256), BF),
-                   sds((C8, Z), F32), sds((16, D), F32)],
+                   sds((4, Z, C8), BF), sds((16, D), F32)],
         scratch_shapes=[
             vm((D, FF), BF), vm((D, FF), BF), vm((T, FF), BF), vm((T, FF), BF), vm((T, D), F32),
             vm((D, T), BF), vm((D, T), BF), vm((D, T), BF), vm((T, D), BF), vm((T, D), BF),
             vm((8, 4, Z, C8), BF), vm((8, 4, R, 256), BF), vm((T, D), BF), vm((T, D), BF), vm((16, D), F32),
             vm((4, 4, Z, C8), BF), vm((2, Z, C8), BF), vm((2, Z, C8), BF), vm((4, Z, C8), BF), vm((4, Z, C8), BF),
-            vm((4, Z, C8), BF),
-            pltpu.SemaphoreType.DMA((n,)), pltpu.SemaphoreType.DMA((n,)), pltpu.SemaphoreType.DMA((6,)),
+            pltpu.SemaphoreType.DMA((n,)), pltpu.SemaphoreType.DMA((n,)), pltpu.SemaphoreType.DMA((12,)),
         ],
         compiler_params=pltpu.CompilerParams(
             collective_id=1, has_side_effects=True, vmem_limit_bytes=62 << 20),
@@ -997,12 +1039,12 @@
 
 
 def third_kernel(length_ref, proj_hbm, qa_hbm, mixed_hbm, dm_hbm, n1_hbm, wp_hbm, x_hbm, dmiddle_hbm, ge_hbm, go_hbm,
-                 vg_ref, v_ref,
-                 tokens_out, gp_out, go_out, ge_out, vec_out,
+                 gc_hbm, vg_ref, v_ref,
+                 tokens_out, gp_out, go_out, ge_out, gc_out, vec_out,
                  proj, qa, mixed, dm, n1, n1t, wpp, x, dmiddle, ge, go, dproj, tg, gp,
                  ka, da, dq, va, kt, vs, vl,
                  lce, lxhe, lyhe, lxe, lye, lze, lco, lxho, lyho, lxo, lyo, lzo,
-                 lcp, lxhp, lyhp, lxp, lyp, lzp, gpw,
+                 lcp, lxhp, lyhp, lxp, lyp, lzp, gpw, gcol, lzc,
                  send_sem, recv_sem, load_sem):
     p = Place()
     T, D = x.shape
@@ -1022,7 +1064,7 @@
         return made
 
     first_loads = [load(a, b) for a, b in ((proj_hbm, proj), (qa_hbm, qa), (mixed_hbm, mixed), (dm_hbm, dm))]
-    ge_load, go_load, n1_load = load(ge_hbm, ge), load(go_hbm, go), load(n1_hbm, n1)
+    ge_load, gc_load, go_load, n1_load = load(ge_hbm, ge), load(gc_hbm, gcol), load(go_hbm, go), load(n1_hbm, n1)
     late = [load(x_hbm, x), load(dmiddle_hbm, dmiddle)]
     for i in range(pairs):
         for s in range(3):
@@ -1036,12 +1078,17 @@
         go_out[...] = jnp.where(p.odd == 0, total[:, 0:192], total[:, 64:256])
 
     rows_of = lambda d: pl.ds(mo(d * R, 16), R)
+    def finish_c(total):
+        gc_out[...] = total
+
+    e_col, o_col = (lambda d: ge.at[rows_of(d), :]), (lambda d: go.at[d])
     e_sib, ev_e = scatter_events(
-        link, p, lambda d: ge.at[rows_of(d), :], lambda ref, h: ref.at[:, pl.ds(h * (FF // 2), FF // 2)],
-        lambda ref, z: ref.at[:, pl.ds(mo(z * Q, 128), Q)], lce, lxhe, lyhe, lxe, lye, lze, finish_e)
+        link, p, e_col, lambda ref, h: ref.at[:, pl.ds(h * (FF // 2), FF // 2)], lce, lxhe, lyhe, lxe, lye)
     o_sib, ev_o = scatter_events(
-        link, p, lambda d: go.at[d], lambda ref, h: ref.at[pl.ds(2 * h, 2)], lambda ref, z: ref.at[z],
-        lco, lxho, lyho, lxo, lyo, lzo, finish_o)
+        link, p, o_col, lambda ref, h: ref.at[pl.ds(2 * h, 2)], lco, lxho, lyho, lxo, lyo)
+    e_send, e_last = z_sum(link, p, lambda z: e_col(p.d).at[:, pl.ds(mo(z * Q, 128), Q)], lze, finish_e)
+    o_send, o_last = z_sum(link, p, lambda z: o_col(p.d).at[z], lzo, finish_o)
+    c_send, c_last = z_sum(link, p, lambda z: gcol.at[z], lzc, finish_c)
     ended = []
     combos = []
     for i in range(pairs):
@@ -1057,8 +1104,8 @@
     def pair_scatter(i):
         column = lambda d: gp.at[i, d]
         sib, events = scatter_events(
-            link, p, column, lambda ref, h: ref.at[pl.ds(h * (R // 2), R // 2)], None,
-            lcp.at[i], lxhp.at[i], lyhp.at[i], lxp.at[i], lyp.at[i], None, None)
+            link, p, column, lambda ref, h: ref.at[pl.ds(h * (R // 2), R // 2)],
+            lcp.at[i], lxhp.at[i], lyhp.at[i], lxp.at[i], lyp.at[i])
         mine = [(at, c) for at, c in enumerate(combos) if c[0] == i]
 
         def along(add_own):
@@ -1120,14 +1167,20 @@
         for i in range(T // 256):
             n1t[:, i * 256:(i + 1) * 256] = n1[i * 256:(i + 1) * 256, :].T
 
-    timeline = [(0, start_e), (1, turn_n1), (3, ev_e[0]), (3, ev_e[1]), (7, ev_e[2]), (7, ev_e[3]), (8, ev_e[4]),
-                (9, start_o), (10, ev_o[0]), (10, ev_o[1]),
-                (14, ev_e[5]), (15, ev_o[2]), (15, ev_o[3]), (15, ev_o[4]), (17, ev_o[5]), (20, ev_o[6]), (21, ev_e[6])]
-    for i in range(pairs - 1):
-        base = max(4 * (i + 1), 9)
-        for k, event in enumerate(ev_p[i]):
-            spot = {0: base, 1: base + 2, 2: base + 2, 3: base + 4, 4: base + 4, 5: base + 4, 6: base + 6, 7: base + 9}[k]
-            timeline.append((spot, event))
+    def start_c():
+        gc_load.wait()
+        c_send()
+
+    e, o = ev_e, ev_o
+    q = ev_p
+    timeline = [
+        (0, start_c), (0, start_e), (1, start_o), (1, turn_n1), (2, e[0]), (3, e[1]), (3, e[4]), (4, q[0][0]), (4, o[0]), (4, o[1]), (4, o[4]),
+        (5, q[0][1]), (5, q[0][2]), (6, q[0][5]), (7, e[2]), (7, e[3]), (8, c_last), (8, o[2]), (8, o[3]), (8, q[1][0]),
+        (9, q[0][3]), (9, q[0][4]), (9, q[1][1]), (9, q[1][2]), (10, q[1][5]), (12, q[2][0]), (13, q[2][1]), (13, q[2][2]),
+        (14, e[5]), (14, e_send), (14, q[2][5]), (16, o[5]), (16, o_send), (16, q[3][0]), (16, q[2][3]), (16, q[2][4]),
+        (16, q[1][3]), (16, q[1][4]), (17, q[0][6]), (17, q[3][1]), (17, q[3][2]), (18, q[3][5]), (19, q[2][6]),
+        (20, q[4][0]), (20, q[3][3]), (20, q[3][4]), (20, q[1][6]), (21, e_last), (21, q[4][1]), (21, q[4][2]),
+        (22, q[4][5]), (22, q[0][7]), (22, q[3][6]), (22, o_last), (23, q[4][3]), (23, q[4][4]), (23, q[1][7]), (23, q[2][7])]
     timeline.sort(key=lambda e: e[0])
 
     def body(step, _):
@@ -1179,7 +1232,6 @@
         return 0
 
     lax.fori_loop(0, pairs * parts, body, 0)
-    tail = [e for at, e in timeline if at >= pairs * parts]
     ev_p[pairs - 1][0]()
     for made in late:
         made.wait()
@@ -1193,8 +1245,9 @@
                 for event in events:
                     event()
 
-        spot(1, ev_p[pairs - 1][1:3])
-        spot(2, ev_p[pairs - 1][3:6])
+        spot(0, q[3][7:8])
+        spot(1, q[5][1:3] + q[5][5:6] + q[4][6:7])
+        spot(3, q[5][3:5] + q[4][7:8])
         r = pl.ds(mo(i * LR, LR), LR)
         left = dproj[r, :]
         dn = dot_nt(left, wpp[...])
@@ -1218,8 +1271,6 @@
     out = load(tg, tokens_out)
     v_slots = [link.slot() for _ in range(6)]
     link.send(v_slots[0], vs, vl.at[0], "c", lambda: vl.at[0])
-    for event in tail:
-        event()
     ev_p[pairs - 1][6]()
     link.got(v_slots[0], vl.at[0])
     vl[6] = vs[...] + vl[0]
@@ -1251,17 +1302,17 @@
     out.wait()
 
 
-def third_call(length, proj, qa, mixed, dm, n1, wp, x, dmiddle, ge, go, vg, v):
+def third_call(length, proj, qa, mixed, dm, n1, wp, x, dmiddle, ge, go, gc, vg, v):
     T, D = x.shape
     FF = ge.shape[1]
     R, Q, pairs = D // 8, FF // 4, H // 2
     vm = pltpu.VMEM
-    n = 12 + 12 + 6 * 12 + 60 + 6
+    n = 8 * 8 + 12 + 60 + 6
     return pl.pallas_call(
         third_kernel,
-        in_specs=[SM] + [ANY] * 10 + [VM] * 2,
-        out_specs=[ANY] + [VM] * 4,
-        out_shape=[sds((T, D), BF), sds((R, 3 * D // 4), F32), sds((R, D // 4), F32), sds((R, Q), F32),
+        in_specs=[SM] + [ANY] * 11 + [VM] * 2,
+        out_specs=[ANY] + [VM] * 5,
+        out_shape=[sds((T, D), BF), sds((R, 3 * D // 4), F32), sds((R, D // 4), F32), sds((R, Q), F32), sds((D // 4, FF // 8), F32),
                    sds((3, 8, 384), F32)],
         scratch_shapes=[
             vm((T, 3 * D), BF), vm((H, T, 128), BF), vm((T, D), BF), vm((T, D), BF), vm((T, D), BF), vm((D, T), BF),
@@ -1274,29 +1325,67 @@
             vm((4, R, 256), BF),
             vm((pairs, 4, R, 384), BF), vm((pairs, R // 2, 384), BF), vm((pairs, R // 2, 384), BF),
             vm((pairs, R, 384), BF), vm((pairs, R, 384), BF), vm((20, 3, R, 128), BF), vm((R, 640), F32),
-            pltpu.SemaphoreType.DMA((n,)), pltpu.SemaphoreType.DMA((n,)), pltpu.SemaphoreType.DMA((28,)),
+            vm((4, D // 4, FF // 8), BF), vm((4, D // 4, FF // 8), BF),
+            pltpu.SemaphoreType.DMA((n,)), pltpu.SemaphoreType.DMA((n,)), pltpu.SemaphoreType.DMA((29,)),
         ],
         compiler_params=pltpu.CompilerParams(
             collective_id=2, has_side_effects=True, vmem_limit_bytes=63 << 20),
         name="third_part",
-    )(length, proj, qa, mixed, dm, n1, wp, x, dmiddle, ge, go, vg, v)
+    )(length, proj, qa, mixed, dm, n1, wp, x, dmiddle, ge, go, gc, vg, v)
+
+
+def last_kernel(block_in, tokens_in, p_in, o_in, e_in, c_in, vec_in,
+                block_out, tokens_out, p_out, o_out, e_out, c_out, *rest):
+    vectors, held, vec, sem = rest[:8], rest[8:14], rest[14], rest[15]
+    parts = 2
+    rows = block_in.shape[0] // parts
+    whole = lambda ref: ref
+    legs = []
+    for i in range(parts):
+        part = lambda ref, i=i: ref.at[pl.ds(i * rows, rows)]
+        legs += [(part, block_in, held[0], block_out), (part, tokens_in, held[1], tokens_out)]
+    legs += [(whole, a, b, c) for a, b, c in zip((p_in, o_in, e_in, c_in), held[2:], (p_out, o_out, e_out, c_out))]
+    first = pltpu.make_async_copy(vec_in, vec, sem.at[2 * len(legs)])
+    first.start()
+    ins = [pltpu.make_async_copy(part(a), part(b), sem.at[k]) for k, (part, a, b, _) in enumerate(legs)]
+    outs = [pltpu.make_async_copy(part(b), part(c), sem.at[len(legs) + k]) for k, (part, _, b, c) in enumerate(legs)]
+    for made in ins:
+        made.start()
+    for came, goes in zip(ins, outs):
+        came.wait()
+        goes.start()
+    first.wait()
+    for at, (i, j) in enumerate(((1, 0), (0, 0), (2, 0), (0, 1), (0, 2), (0, 3), (0, 4), (0, 5))):
+        n = vectors[at].shape[0]
+        vectors[at][...] = vec[i, j:j + 1, 0:n].reshape(n)
+    for goes in outs:
+        goes.wait()
+
+
+def last_call(sizes, *arrays):
+    return pl.pallas_call(
+        last_kernel,
+        in_specs=[ANY] * 7,
+        out_specs=[ANY] * 6 + [VM] * 8,
+        out_shape=[sds(item.shape, item.dtype) for item in arrays[:6]] + [sds((n,), F32) for n in sizes],
+        scratch_shapes=[pltpu.VMEM(item.shape, item.dtype) for item in arrays] + [pltpu.SemaphoreType.DMA((17,))],
+        compiler_params=pltpu.CompilerParams(vmem_limit_bytes=63 << 20),
+        name="last_part",
+    )(*arrays)
 
 
 def per_device_fast(tokens, lengths, cotangent, project_weight, project_bias, output_weight, output_bias,
                     expand_weight, expand_bias, contract_weight, contract_bias, first_gain, first_shift,
                     second_gain, second_shift):
-    vec = pack_vectors(project_bias, output_bias, expand_bias, contract_bias,
-                       first_gain, first_shift, second_gain, second_shift)
-    normed_one, projected, mixed, qa, full_project, full_output, full_expand, v = first_call(
-        lengths, tokens, project_weight, output_weight, expand_weight, vec)
-    block_out, grad_mixed, grad_middle, ge, go, grad_contract, vg = second_call(
-        lengths, tokens, cotangent, mixed, full_output, full_expand, contract_weight, v)
-    tokens_grad, grad_project, grad_output, grad_expand, vo = third_call(
-        lengths, projected, qa, mixed, grad_mixed, normed_one, full_project, tokens, grad_middle, ge, go, vg, v)
-    r = output_bias.shape[0]
-    return (block_out, tokens_grad, grad_project, vo[1, 0, :2 * r], grad_output, vo[0, 0, :r],
-            grad_expand, vo[2, 0, :4 * r], grad_contract, vo[0, 1, :r],
-            vo[0, 2, :r], vo[0, 3, :r], vo[0, 4, :r], vo[0, 5, :r])
+    vectors = (project_bias, output_bias, expand_bias, contract_bias, first_gain, first_shift, second_gain, second_shift)
+    normed_one, projected, mixed, qa, full_project, full_output, full_expand, cc, v = first_call(
+        lengths, tokens, project_weight, output_weight, expand_weight, contract_weight.T, vectors)
+    block_out, grad_mixed, grad_middle, ge, go, gc, vg = second_call(
+        lengths, tokens, cotangent, mixed, full_output, full_expand, cc, v)
+    third = third_call(
+        lengths, projected, qa, mixed, grad_mixed, normed_one, full_project, tokens, grad_middle, ge, go, gc, vg, v)
+    out = last_call([item.shape[0] for item in vectors], block_out, *third)
+    return (out[0], out[1], out[2], out[6], out[3], out[7], out[4], out[8], out[5].T, *out[9:])
 
 
 def solution(mesh):

time: 295 us -> 245 us (0.83)
  Pallas kernels: 274 us -> 243 us
  local copies, waits for them, and re-layouts: 18.6 us -> 0 us
    pallas_call x3 -> x4, Pallas kernels: 274 us -> 243 us  [the longest x1 90.5 us: third_call(): pl.pallas_call(third_kernel, in_specs=[SM] + [ANY] * 11 + [VM] * 2, out_s...]
    unnamed x17 -> x0, local copies, waits for them, and re-layouts: 8.57 us -> none
    pad x8 -> x0, local copies, waits for them, and re-layouts: 5.22 us -> none  [the longest x7 4.62 us: pack_vectors(): jnp.pad(v, (0, wide - v.shape[0]))]
where the time goes in v3:
time: 245 us
  Pallas kernels  243 us (99%)
    pallas_call x1, Pallas kernels, third_call(): pl.pallas_call(third_kernel, in_specs=[SM] + [ANY] * 11 + [VM] * 2, out_s...  90.5 us
    pallas_call x1, Pallas kernels, first_call(): pl.pallas_call(first_kernel, in_specs=[S] + [V] * 13, out_specs=[ANY] * 9...  84.9 us
    pallas_call x1, Pallas kernels, second_call(): pl.pallas_call(second_kernel, in_specs=[SM, VM, VM, VM, VM, ANY, ANY, VM]...  63.8 us

profile of v3, /device:TPU:0, one launch (start us, length us, event | category | flops | bytes accessed | tf_op | source)
XLA Modules:
  0.0 244.6 jit_solution(15135045824477687694)
XLA Ops:
  1.3 84.9 %first_part.1 = (bf16[1024,768]{1,0:T(8,128)(2,1)}, bf16[1024,2304]{1,0:T(8,128)(2,1)}, bf16[1024,768]{1,0:T(8,128)(2,1)}, bf16[12,1024,128]{2,1,0:T(8,128)(2,1)...) custom-call(s32[1]{0:T(128)S(6)} %copy.29.length_ref, ...), custom_call_target="tpu_custom_call" | custom-call | tf_op jit(solution)/shard_map/first_part/pallas_call | solution.py:418
  86.2 63.8 %second_part.1 = (bf16[1024,768]{1,0:T(8,128)(2,1)}, bf16[1024,768]{1,0:T(8,128)(2,1)}, f32[1024,768]{1,0:T(8,128)}, bf16[768,3072]{1,0:T(8,128)(2,1)}, bf16[8,4...) custom-call(s32[1]{0:T(128)S(6)} %copy.29.length_ref, bf16[1024,768]{1,0:T(8,128)(2,1)} %x_hbm.1, ...), custom_call_target="tpu_custom_call" | custom-call | tf_op jit(solution)/shard_map/second_part/pallas_call | solution.py:1022
  150.0 90.5 %third_part.1 = (bf16[1024,768]{1,0:T(8,128)(2,1)}, f32[96,576]{1,0:T(8,128)}, f32[96,192]{1,0:T(8,128)}, f32[96,768]{1,0:T(8,128)}, f32[192,384]{1,0:T(8,128)}, /*index=5*/f32[3,8,384]{2,1,0:T(8,128)}) custom-call(s32[1]{0:T(128)S(6)} %copy.29.length_ref, bf16[1024,2304]{1,0:T(8,128)(2,1)} %get-tuple-element.56.proj_hbm, ...), custom_call_target="tpu_custom_call" | custom-call | tf_op jit(solution)/shard_map/third_part/pallas_call | solution.py:1311
  240.5 3.9 %last_part.1 = (bf16[1024,768]{1,0:T(8,128)(2,1)}, bf16[1024,768]{1,0:T(8,128)(2,1)}, f32[96,576]{1,0:T(8,128)}, f32[96,192]{1,0:T(8,128)}, f32[96,768]{1,0:T(8,...) custom-call(bf16[1024,768]{1,0:T(8,128)(2,1)} %get-tuple-element.55., ...), custom_call_target="tpu_custom_call" | custom-call | tf_op jit(solution)/shard_map/last_part/pallas_call | solution.py:1366
